TPU v7x, 512 devices: a whole 4x8x8 slice. The times are simulated.
512 devices in a mesh: dp: 64 (over z_hi, y, x), fsdp: 8 (over z_lo, core).
Axes of the slice: x: 4, y: 8, z: 8 (z_hi: 2, z_lo: 4; z = z_hi * 4 + z_lo), core: 2. Of those that a mesh axis runs over, the one named last changes fastest.
Arguments:
- activations: bfloat16 [24576, 4096], P('dp', 'fsdp'), may hold values from -16 to 16
- grad_out: bfloat16 [24576, 14336], P('dp', 'fsdp'), may hold values from -0.0234375 to 0.0234375
- projector: bfloat16 [1024, 14336], P('dp', 'fsdp'), may hold values from -0.1875 to 0.1875
- weight: bfloat16 [8, 512, 14336], P(None, 'dp', 'fsdp'), may hold values from -6 to 6
- moment_one_in: float32 [8, 512, 1024], P('fsdp', 'dp'), may hold values from -6 to 6
- moment_two_in: float32 [8, 512, 1024], P('fsdp', 'dp'), may hold values from 0.25 to 4
Outputs:
- new_weight: bfloat16 [8, 512, 14336], P(None, 'dp')
- moment_one: float32 [8, 512, 1024], P('fsdp', 'dp')
- moment_two: float32 [8, 512, 1024], P('fsdp', 'dp')
All inputs are finite; a program needn't handle non-finite values.
Results may differ from a plain program's by a relative error of at most 0.003.
Values may be sent and summed in bfloat16 or wider, within the bound.
No kernel may reach another device: no remote copies, remote signals or barrier semaphores. Data moves between devices by JAX's collectives and lax.ppermute only.
A program may use at most 64 MiB of HBM per device.

v0:
```python
import jax
import jax.numpy as jnp
from jax import lax
from jax.sharding import PartitionSpec as P

decay_first = 0.9
decay_second = 0.95
bias_first = 1.0 / (1.0 - 0.9**10)
bias_second = 1.0 / (1.0 - 0.95**10)
step_scale = 0.25
epsilon = 1e-08


def sweep_basis(projector, combine, start_value):
    return combine(start_value, lax.all_gather(projector, "dp", axis=0, tiled=True), jnp.int32(0))


def contract_last(left, right):
    return lax.dot_general(
        left, right, (((1,), (1,)), ((), ())), preferred_element_type=jnp.float32
    )


def shards(activations, grad_out, projector, weight, moment_one_in, moment_two_in):
    tok_rows = grad_out.shape[0]
    rank_total = projector.shape[0] * lax.axis_size("dp")
    ff_local = projector.shape[1]

    def project(running, shard_rows, offset):
        product = contract_last(grad_out, shard_rows)
        return product

    summand = sweep_basis(projector, project, jnp.zeros((tok_rows, rank_total), jnp.float32))
    projected = lax.psum(summand, "fsdp").astype(jnp.bfloat16)
    low_grad = lax.psum_scatter(
        lax.dot_general(
            activations, projected, (((0,), (0,)), ((), ())), preferred_element_type=jnp.float32
        ),
        "dp",
        scatter_dimension=0,
        tiled=True,
    ).reshape(moment_one_in.shape)
    moment_one = decay_first * moment_one_in + (1.0 - decay_first) * low_grad
    moment_two = decay_second * moment_two_in + (1.0 - decay_second) * low_grad * low_grad
    direction = (bias_first * moment_one / (jnp.sqrt(bias_second * moment_two) + epsilon)).astype(
        jnp.bfloat16
    )
    gathered = lax.all_gather(direction, "fsdp", axis=0, tiled=True)
    stacked = gathered.reshape(-1, rank_total)

    def unproject(running, shard_rows, offset):
        return jnp.dot(stacked, shard_rows, preferred_element_type=jnp.float32)

    update = sweep_basis(projector, unproject, jnp.zeros((stacked.shape[0], ff_local), jnp.float32))
    updated = (weight.astype(jnp.float32) - step_scale * update.reshape(weight.shape)).astype(
        jnp.bfloat16
    )
    new_weight = lax.all_gather(updated, "fsdp", axis=2, tiled=True)
    return (new_weight, moment_one, moment_two)


def solution(mesh):
    in_specs = (
        P("dp", "fsdp"),
        P("dp", "fsdp"),
        P("dp", "fsdp"),
        P(None, "dp", "fsdp"),
        P("fsdp", "dp", None),
        P("fsdp", "dp", None),
    )
    out_specs = (P(None, "dp", None), P("fsdp", "dp", None), P("fsdp", "dp", None))
    return jax.shard_map(shards, mesh=mesh, in_specs=in_specs, out_specs=out_specs, check_vma=False)
```

profile of v0, /device:TPU:1, one launch (start us, length us, event | category | flops | bytes accessed | tf_op | source)
XLA Modules:
  0.0 736.1 jit_solution(14573585380136302620)
XLA Ops:
  7.2 0.0 copy-start
  7.2 0.0 all-gather.3.cloned.1.call-start
  7.2 0.7 all-gather.3.cloned.1.call-update
  7.9 0.0 reduce-scatter.4.cloned.1.call-start
  8.0 159.4 %all-gather.3.cloned.1.call-done = bf16[1024,1792]{1,0:T(8,128)(2,1)} async-done(((bf16[16,1792]{1,0:T(8,128)(2,1)}), bf16[1024,1792]{1,0:T(8,128)(2,1)}) %all-gather.3.cloned.1.call-update) | async-done | bytes 3670032 | tf_op jit(solution)/shard_map/all_gather | solution.py:15
  167.3 0.0 copy-done
  167.3 3.6 fusion.15
  171.0 60.1 %all-reduce.1 = bf16[384,1024]{1,0:T(8,128)(2,1)} all-reduce(f32[384,1024]{1,0:T(8,128)S(1)} %fusion.15), channel_id=1, replica_groups=mesh['dp'=64,'fsdp'=8] {'fsdp'}, use_global_device_ids=true, to_apply=%region_0.0 | all-reduce | flops 393216 | bytes 2359296 | tf_op jit(solution)/shard_map/psum | solution.py:34
  231.1 2.0 convolution_bitcast_fusion
  233.0 1.9 copy.27
  234.9 0.0 copy-start.2
  234.9 0.0 copy-start.3
  234.9 0.0 copy-start.1
  234.9 0.0 reduce-scatter.4.cloned.1.call-update
  234.9 0.0 all-gather.5.cloned.1.call-start
  235.0 391.7 %reduce-scatter.4.cloned.1.call-done = f32[8,1024]{1,0:T(8,128)} async-done(((f32[512,1024]{1,0:T(8,128)}), f32[8,1024]{1,0:T(8,128)}) %reduce-scatter.4.cloned.1.call-update) | async-done | bytes 32784 | tf_op jit(solution)/shard_map/reduce_scatter | solution.py:35
  626.7 0.0 copy-done.2
  626.7 0.0 copy-done.3
  626.7 1.4 divide_convert_fusion
  628.1 66.3 %all_gather.11 = bf16[8,8,1024]{2,1,0:T(8,128)(2,1)S(1)} all-gather(bf16[1,8,1024]{2,1,0:T(8,128)(2,1)S(1)} %get-tuple-element.9), channel_id=1, replica_groups=mesh['dp'=64,'fsdp'=8] {'fsdp'}, dimensions={0}, use_global_device_ids=true | all-gather | bytes 147456 | tf_op jit(solution)/shard_map/all_gather | solution.py:48
  694.4 0.0 copy-done.1
  694.4 3.5 fusion.8
  697.9 0.0 all-gather.5.cloned.1.call-update
  697.9 28.9 %all-gather.5.cloned.1.call-done = bf16[8,8,14336]{2,1,0:T(8,128)(2,1)} async-done(((bf16[8,8,1792]{2,1,0:T(8,128)(2,1)}), bf16[8,8,14336]{2,1,0:T(8,128)(2,1)}) %all-gather.5.cloned.1.call-update) | async-done | bytes 1835024 | tf_op jit(solution)/shard_map/all_gather | solution.py:58
  726.8 2.8 copy.32
Async XLA Ops:
  7.2 160.2 %copy-start = (bf16[384,1792]{1,0:T(8,128)(2,1)S(1)}, bf16[384,1792]{1,0:T(8,128)(2,1)}, u32[]{:S(2)}) copy-start(bf16[384,1792]{1,0:T(8,128)(2,1)} %param.7) | copy-start | bytes 4128772
  7.2 160.1 %all-gather.3.cloned.1.call-start = ((), (), s32[]{:S(2)}) async-start(), calls=%async_computation.1 | async-start | bytes 3727360 | tf_op jit(solution)/shard_map/all_gather | solution.py:15
  7.9 618.8 %reduce-scatter.4.cloned.1.call-start = ((), (), s32[]{:S(2)}) async-start(), calls=%async_computation.3 | async-start | bytes 2129920 | tf_op jit(solution)/shard_map/reduce_scatter | solution.py:35
  234.9 391.8 %copy-start.2 = (f32[1,8,1024]{2,1,0:T(8,128)S(1)}, f32[1,8,1024]{2,1,0:T(8,128)}, u32[]{:S(2)}) copy-start(f32[1,8,1024]{2,1,0:T(8,128)} %param.10) | copy-start | bytes 98308
  234.9 391.8 %copy-start.3 = (f32[1,8,1024]{2,1,0:T(8,128)S(1)}, f32[1,8,1024]{2,1,0:T(8,128)}, u32[]{:S(2)}) copy-start(f32[1,8,1024]{2,1,0:T(8,128)} %param.11) | copy-start | bytes 98308
  234.9 459.5 %copy-start.1 = (bf16[8,8,1792]{2,1,0:T(8,128)(2,1)S(1)}, bf16[8,8,1792]{2,1,0:T(8,128)(2,1)}, u32[]{:S(2)}) copy-start(bf16[8,8,1792]{2,1,0:T(8,128)(2,1)} %param.9) | copy-start | bytes 688132
  234.9 491.9 %all-gather.5.cloned.1.call-start = ((), (), s32[]{:S(2)}) async-start(), calls=%async_computation.2 | async-start | bytes 2064384 | tf_op jit(solution)/shard_map/all_gather | solution.py:58
Sparse Core Ops, SparseCore 0:
  12.5 154.7 all-gather.2
  235.0 391.6 reduce-scatter.3
  698.0 28.6 all-gather.4
where the time goes:
time: 737 us; the launch traced here: 736 us
  waiting for transfers between devices  581 us (79%)
  blocking collectives  126 us (17%)
  between operations  13.8 us (2%)
  matrix products  9.1 us (1%)
    reduce_scatter x1, waiting for transfers between devices, shards(): lax.psum_scatter(lax.dot_general(activations, projected, (((0,), (0,)), (...  392 us
    all_gather x1, waiting for transfers between devices, sweep_basis(): lax.all_gather(projector, 'dp', axis=0, tiled=True)  159 us
    all_gather x1, blocking collectives, shards(): gathered = lax.all_gather(direction, 'fsdp', axis=0, tiled=True)  66.3 us
    psum x1, blocking collectives, shards(): projected = lax.psum(summand, 'fsdp').astype(jnp.bfloat16)  60.1 us
    all_gather x1, waiting for transfers between devices, shards(): new_weight = lax.all_gather(updated, 'fsdp', axis=2, tiled=True)  28.9 us
  transfers between devices with their start and end apart: 3, of which 3 were waited for; matrix products, arithmetic and copies ran while one was open for 0% of the time, Pallas kernels for 0%

commit v1 on v0

v1 whole, which is shorter than its diff:
```python
import jax
import jax.numpy as jnp
from jax import lax
from jax.sharding import Mesh, PartitionSpec as P

decay_first = 0.9
decay_second = 0.95
bias_first = 1.0 / (1.0 - 0.9**10)
bias_second = 1.0 / (1.0 - 0.95**10)
step_scale = 0.25
epsilon = 1e-08

fine_axes = ("zh", "y", "x", "zl", "core")
fine_sizes = (2, 8, 4, 4, 2)
dp = ("zh", "y", "x")
rest = ("zh", "y")
fsdp = ("zl", "core")


def gather(block, axes):
    return lax.all_gather(block, axes, axis=0, tiled=True)


def exchange(block, axes):
    return lax.all_to_all(block, axes, 0, 0, tiled=True)


def contract(left, right, dims):
    return lax.dot_general(left, right, (dims, ((), ())), preferred_element_type=jnp.float32)


def summed(pieces):
    return jnp.sum(pieces.astype(jnp.float32), axis=0)


def ranks_by_x(moment):
    rows, ranks = moment.shape
    return moment.reshape(rows, 2, 8, 4, 16).transpose(0, 3, 2, 1, 4).reshape(rows, ranks)


def ranks_in_order(moment):
    rows, ranks = moment.shape
    return moment.reshape(rows, 4, 8, 2, 16).transpose(0, 3, 2, 1, 4).reshape(rows, ranks)


def shards(activations, grad_out, projector, weight, moment_one_in, moment_two_in):
    blocks, rows, ff_local = weight.shape
    rank_total = moment_one_in.shape[2]

    tokens_grad = gather(grad_out, "x")
    quarter = gather(gather(projector, "zh"), "y")
    tokens_act = gather(activations, "x")
    basis = gather(quarter, "x")
    first_in = ranks_by_x(moment_one_in[0])
    second_in = ranks_by_x(moment_two_in[0])

    partial = contract(tokens_grad, quarter, ((1,), (1,))).astype(jnp.bfloat16)
    tokens, ranks = partial.shape
    pieces = exchange(partial.reshape(8, tokens // 8, ranks), fsdp)
    projected = gather(summed(pieces).astype(jnp.bfloat16), fsdp)

    low = contract(tokens_act, projected, ((0,), (0,))).astype(jnp.bfloat16)
    pieces = exchange(low.reshape(16, low.shape[0] // 16, ranks), rest)
    low = summed(pieces)
    low = exchange(low.reshape(4, rows, ranks), "x")
    low_grad = low.transpose(1, 0, 2).reshape(rows, rank_total)

    moment_one = decay_first * first_in + (1.0 - decay_first) * low_grad
    moment_two = decay_second * second_in + (1.0 - decay_second) * low_grad * low_grad
    direction = (bias_first * moment_one / (jnp.sqrt(bias_second * moment_two) + epsilon)).astype(
        jnp.bfloat16
    )
    copies = jnp.broadcast_to(direction[None], (8, rows, rank_total))
    stacked = exchange(copies, fsdp).reshape(blocks * rows, rank_total)

    update = contract(stacked, basis, ((1,), (0,)))
    updated = (weight.astype(jnp.float32) - step_scale * update.reshape(weight.shape)).astype(
        jnp.bfloat16
    )
    column = gather(updated[None], "zl")
    halves = [
        lax.all_gather(column[:, part * 4 : part * 4 + 4], "core", axis=1) for part in range(2)
    ]
    both = jnp.concatenate(halves, axis=2)
    new_weight = both.transpose(2, 3, 0, 1, 4).reshape(blocks, rows, 8 * ff_local)
    return (
        new_weight,
        ranks_in_order(moment_one)[None],
        ranks_in_order(moment_two)[None],
    )


def solution(mesh):
    fine = Mesh(mesh.devices.reshape(fine_sizes), fine_axes)
    in_specs = (
        P(dp, fsdp),
        P(dp, fsdp),
        P(dp, fsdp),
        P(None, dp, fsdp),
        P(fsdp, dp, None),
        P(fsdp, dp, None),
    )
    out_specs = (P(None, dp, None), P(fsdp, dp, None), P(fsdp, dp, None))
    return jax.shard_map(shards, mesh=fine, in_specs=in_specs, out_specs=out_specs, check_vma=False)
```

time: 737 us -> 210 us (0.28)
  waiting for transfers between devices: 581 us -> 54.9 us
  blocking collectives: 126 us -> 104 us
  starting transfers between devices: 0.12 us -> 20 us
    reduce_scatter x1 -> x0, waiting for transfers between devices: 392 us -> none  [shards(): lax.psum_scatter(lax.dot_general(activations, projected, (((0,), (0,)), (...]
    all_gather x2 -> x3, waiting for transfers between devices: 188 us -> 34 us  [gather(): return lax.all_gather(block, axes, axis=0, tiled=True)]
    psum x1 -> x0, blocking collectives: 60.1 us -> none  [shards(): projected = lax.psum(summand, 'fsdp').astype(jnp.bfloat16)]
    all_to_all x0 -> x1, blocking collectives: none -> 25.9 us  [exchange(): return lax.all_to_all(block, axes, 0, 0, tiled=True)]
    all_to_all x0 -> x3, starting transfers between devices: none -> 19.9 us  [exchange(): return lax.all_to_all(block, axes, 0, 0, tiled=True)]
    all_to_all x0 -> x3, waiting for transfers between devices: none -> 19.5 us  [exchange(): return lax.all_to_all(block, axes, 0, 0, tiled=True)]
    all_gather x1 -> x6, blocking collectives: 66.3 us -> 77.7 us  [the longest x4 70.8 us: gather(): return lax.all_gather(block, axes, axis=0, tiled=True)]
  transfers between devices with their start and end apart: 3 -> 6, of which waited for: 3 -> 4; matrix products, arithmetic and copies ran while one was open for 0% -> 6% of each run, Pallas kernels for 0% -> 0%
where the time goes in v1:
time: 210 us
  blocking collectives  104 us (50%)
  waiting for transfers between devices  54.9 us (26%)
  starting transfers between devices  20 us (10%)
  between operations  13.9 us (7%)
  matrix products  9.22 us (4%)
  local copies, waits for them, and re-layouts  6.65 us (3%)
    all_gather x4, blocking collectives, gather(): return lax.all_gather(block, axes, axis=0, tiled=True)  70.8 us
    all_gather x3, waiting for transfers between devices, gather(): return lax.all_gather(block, axes, axis=0, tiled=True)  34 us
    all_to_all x1, blocking collectives, exchange(): return lax.all_to_all(block, axes, 0, 0, tiled=True)  25.9 us
    all_to_all x3, starting transfers between devices, exchange(): return lax.all_to_all(block, axes, 0, 0, tiled=True)  19.9 us
    all_to_all x3, waiting for transfers between devices, exchange(): return lax.all_to_all(block, axes, 0, 0, tiled=True)  19.5 us
    dot_general x3, matrix products, contract(): lax.dot_general(left, right, (dims, ((), ())), preferred_element_type=jnp...  9.22 us
    all_gather x2, blocking collectives, shards(): lax.all_gather(column[:, part * 4:part * 4 + 4], 'core', axis=1)  6.83 us
  transfers between devices with their start and end apart: 6, of which 4 were waited for; matrix products, arithmetic and copies ran while one was open for 6% of the time, Pallas kernels for 0%

profile of v1, /device:TPU:1, one launch (start us, length us, event | category | flops | bytes accessed | tf_op | source)
XLA Modules:
  0.0 209.5 jit_solution(14106301498734238512)
XLA Ops:
  7.2 0.0 all-gather.7.cloned.1.call-start
  7.2 0.7 all-gather.7.cloned.1.call-update
  7.9 0.0 all-gather.9.cloned.1.call-start
  7.9 0.7 all-gather.9.cloned.1.call-update
  8.6 0.0 all-gather.11.cloned.1.call-start
  8.7 12.1 %all_gather.34 = bf16[32,1792]{1,0:T(8,128)(2,1)S(1)} all-gather(bf16[16,1792]{1,0:T(8,128)(2,1)} %param.8), channel_id=1, replica_groups=mesh['zh'=2,'y'=8,'x'=4,'zl'=4,'core'=2] {'zh'}, dimensions={0}, use_global_device_ids=true | all-gather | bytes 172032 | tf_op jit(solution)/shard_map/all_gather | solution.py:21
  20.8 25.2 %all_gather.35 = bf16[256,1792]{1,0:T(8,128)(2,1)} all-gather(bf16[32,1792]{1,0:T(8,128)(2,1)S(1)} %all_gather.34), channel_id=1, replica_groups=mesh['zh'=2,'y'=8,'x'=4,'zl'=4,'core'=2] {'y'}, dimensions={0}, use_global_device_ids=true | all-gather | bytes 1032192 | tf_op jit(solution)/shard_map/all_gather | solution.py:21
  46.0 0.0 all-gather.11.cloned.1.call-update
  46.0 34.0 %all-gather.7.cloned.1.call-done = bf16[1536,1792]{1,0:T(8,128)(2,1)} async-done(((bf16[384,1792]{1,0:T(8,128)(2,1)}), bf16[1536,1792]{1,0:T(8,128)(2,1)}) %all-gather.7.cloned.1.call-update) | async-done | bytes 5505040 | tf_op jit(solution)/shard_map/all_gather | solution.py:21
  80.1 4.4 %convolution_convert_fusion = bf16[1536,256]{1,0:T(8,128)(2,1)S(1)} fusion(bf16[1536,1792]{1,0:T(8,128)(2,1)} %all-gather.7.cloned.1.call-done, bf16[256,1792]{1,0:T(8,128)(2,1)} %all_gather.35), kind=kOutput, calls=%fused_computation.2 | convolution fusion | flops 1409679360 | bytes 7208960 | tf_op jit(solution)/shard_map/dot_general | solution.py:29
  84.5 25.9 %all_to_all.20 = bf16[8,192,256]{2,1,0:T(8,128)(2,1)S(1)} all-to-all(bf16[8,192,256]{2,1,0:T(8,128)(2,1)S(1)} %bitcast.47), channel_id=1, replica_groups=mesh['zh'=2,'y'=8,'x'=4,'zl'=4,'core'=2] {'zl','core'}, dimensions={0} | all-to-all | bytes 1572864 | tf_op jit(solution)/shard_map/all_to_all | solution.py:25
  110.4 0.1 reduce_sum.21
  110.5 15.7 %all_gather.36 = bf16[1536,256]{1,0:T(8,128)(2,1)S(1)} all-gather(bf16[192,256]{1,0:T(8,128)(2,1)S(1)} %reduce_sum.21), channel_id=1, replica_groups=mesh['zh'=2,'y'=8,'x'=4,'zl'=4,'core'=2] {'zl','core'}, dimensions={0}, use_global_device_ids=true | all-gather | bytes 884736 | tf_op jit(solution)/shard_map/all_gather | solution.py:21
  126.3 0.0 copy-start.1
  126.3 0.0 copy-start.2
  126.3 0.0 all-gather.9.cloned.1.call-done
  126.3 2.0 fusion.11
  128.3 0.8 copy.33
  129.1 9.7 %all-to-all-start.1 = ((bf16[16,32,256]{2,1,0:T(8,128)(2,1)}), bf16[16,32,256]{2,1,0:T(8,128)(2,1)S(1)}, u32[]{:S(2)}, u32[]{:S(2)}) async-start(bf16[16,32,256]{2,1,0:T(8,128)(2,1)} %bitcast.3), calls=%async_computation.1 | async-start | bytes 524288 | tf_op jit(solution)/shard_map/all_to_all | solution.py:25
  138.9 0.0 copy-done.1
  138.9 13.0 %all-to-all-done.1 = bf16[16,32,256]{2,1,0:T(8,128)(2,1)S(1)} async-done(((bf16[16,32,256]{2,1,0:T(8,128)(2,1)}), bf16[16,32,256]{2,1,0:T(8,128)(2,1)S(1)}, u32[]{:S(2)}, u32[]{:S(2)}) %all-to-all-start.1) | async-done | bytes 262176 | tf_op jit(solution)/shard_map/all_to_all | solution.py:25
  151.9 0.7 convert_reduce_fusion
  152.5 3.6 %all-to-all-start.2 = ((f32[4,8,256]{2,1,0:T(8,128)}), f32[4,8,256]{2,1,0:T(8,128)S(1)}, u32[]{:S(2)}, u32[]{:S(2)}) async-start(f32[4,8,256]{2,1,0:T(8,128)} %bitcast.4), calls=%async_computation.2 | async-start | bytes 65536 | tf_op jit(solution)/shard_map/all_to_all | solution.py:25
  156.2 0.0 copy-done.2
  156.2 0.2 mul.121
  156.4 0.1 copy.35
  156.6 0.3 mul.123
  156.9 0.2 mul.112
  157.1 0.2 copy.32
  157.4 0.0 copy-start
  157.4 0.3 mul.114
  157.7 3.1 %all-to-all-done.2 = f32[4,8,256]{2,1,0:T(8,128)S(1)} async-done(((f32[4,8,256]{2,1,0:T(8,128)}), f32[4,8,256]{2,1,0:T(8,128)S(1)}, u32[]{:S(2)}, u32[]{:S(2)}) %all-to-all-start.2) | async-done | bytes 32800 | tf_op jit(solution)/shard_map/all_to_all | solution.py:25
  160.9 0.7 broadcast_in_dim.4
  161.5 6.6 %all-to-all-start.3 = ((bf16[8,8,1024]{2,1,0:T(8,128)(2,1)}), bf16[8,8,1024]{2,1,0:T(8,128)(2,1)S(1)}, u32[]{:S(2)}, u32[]{:S(2)}) async-start(bf16[8,8,1024]{2,1,0:T(8,128)(2,1)} %broadcast_in_dim.4), calls=%async_computation.3 | async-start | bytes 262144 | tf_op jit(solution)/shard_map/all_to_all | solution.py:25
  168.1 0.4 reshape.81
  168.6 0.1 copy.41
  168.7 0.9 broadcast_in_dim_reshape.7
  169.5 0.2 fusion.15
  169.8 0.9 broadcast_in_dim_reshape.6
  170.6 3.3 %all-to-all-done.3 = bf16[8,8,1024]{2,1,0:T(8,128)(2,1)S(1)} async-done(((bf16[8,8,1024]{2,1,0:T(8,128)(2,1)}), bf16[8,8,1024]{2,1,0:T(8,128)(2,1)S(1)}, u32[]{:S(2)}, u32[]{:S(2)}) %all-to-all-start.3) | async-done | bytes 131104 | tf_op jit(solution)/shard_map/all_to_all | solution.py:25
  174.0 0.0 copy-done
  174.0 2.8 %fusion.8 = bf16[8,8,1792]{2,1,0:T(8,128)(2,1)S(1)} fusion(bf16[8,8,1024]{2,1,0:T(8,128)(2,1)S(1)} %all-to-all-done.3, bf16[1024,1792]{1,0:T(8,128)(2,1)} %all-gather.11.cloned.1.call-done, bf16[8,8,1792]{2,1,0:T(8,128)(2,1)S(1)} %copy-done), kind=kOutput, calls=%fused_computation.5 | convolution fusion | flops 235339776 | bytes 4259840 | tf_op jit(solution)/shard_map/dot_general | solution.py:29
  176.8 17.8 %all-gather = bf16[32,8,1792]{2,1,0:T(8,128)(2,1)S(1)} all-gather(bf16[8,8,1792]{2,1,0:T(8,128)(2,1)S(1)} %fusion.8), channel_id=2, replica_groups=mesh['zh'=2,'y'=8,'x'=4,'zl'=4,'core'=2] {'zl'}, dimensions={0}, use_global_device_ids=true | all-gather | bytes 1146880 | tf_op jit(solution)/shard_map/all_gather | solution.py:21
  194.6 0.1 fusion.22
  194.6 4.4 %all-gather.1 = bf16[4,8,8,1792]{3,2,1,0:T(8,128)(2,1)S(1)} all-gather(bf16[4,4,8,1792]{3,2,1,0:T(8,128)(2,1)S(1)} %get-tuple-element.3), channel_id=3, replica_groups=mesh['zh'=2,'y'=8,'x'=4,'zl'=4,'core'=2] {'core'}, dimensions={1}, use_global_device_ids=true | all-gather | bytes 1376256 | tf_op jit(solution)/shard_map/all_gather | solution.py:82
  199.0 2.5 %all-gather.2 = bf16[4,8,8,1792]{3,2,1,0:T(8,128)(2,1)S(1)} all-gather(bf16[4,4,8,1792]{3,2,1,0:T(8,128)(2,1)S(1)} %get-tuple-element.4), channel_id=4, replica_groups=mesh['zh'=2,'y'=8,'x'=4,'zl'=4,'core'=2] {'core'}, dimensions={1}, use_global_device_ids=true | all-gather | bytes 1376256 | tf_op jit(solution)/shard_map/all_gather | solution.py:82
  201.4 0.2 pad_maximum_fusion
  201.6 1.4 copy.42
  (6 shorter events, 0.1 us)
Async XLA Ops:
  7.2 72.9 %all-gather.7.cloned.1.call-start = ((), (), s32[]{:S(2)}) async-start(), calls=%async_computation.4 | async-start | bytes 6881280 | tf_op jit(solution)/shard_map/all_gather | solution.py:21
  7.9 118.4 %all-gather.9.cloned.1.call-start = ((), (), s32[]{:S(2)}) async-start(), calls=%async_computation.5 | async-start | bytes 1966080 | tf_op jit(solution)/shard_map/all_gather | solution.py:21
  8.6 162.0 %all-gather.11.cloned.1.call-start = ((), (), s32[]{:S(2)}) async-start(), calls=%async_computation.6 | async-start | bytes 4587520 | tf_op jit(solution)/shard_map/all_gather | solution.py:21
  126.3 12.6 %copy-start.1 = (f32[1,8,1024]{2,1,0:T(8,128)S(1)}, f32[1,8,1024]{2,1,0:T(8,128)}, u32[]{:S(2)}) copy-start(f32[1,8,1024]{2,1,0:T(8,128)} %param.11) | copy-start | bytes 98308
  126.3 29.9 %copy-start.2 = (f32[1,8,1024]{2,1,0:T(8,128)S(1)}, f32[1,8,1024]{2,1,0:T(8,128)}, u32[]{:S(2)}) copy-start(f32[1,8,1024]{2,1,0:T(8,128)} %param.10) | copy-start | bytes 98308
  129.1 22.7 %all-to-all-start.1 = ((bf16[16,32,256]{2,1,0:T(8,128)(2,1)}), bf16[16,32,256]{2,1,0:T(8,128)(2,1)S(1)}, u32[]{:S(2)}, u32[]{:S(2)}) async-start(bf16[16,32,256]{2,1,0:T(8,128)(2,1)} %bitcast.3), calls=%async_computation.1 | async-start | bytes 524288 | tf_op jit(solution)/shard_map/all_to_all | solution.py:25
  152.5 8.3 %all-to-all-start.2 = ((f32[4,8,256]{2,1,0:T(8,128)}), f32[4,8,256]{2,1,0:T(8,128)S(1)}, u32[]{:S(2)}, u32[]{:S(2)}) async-start(f32[4,8,256]{2,1,0:T(8,128)} %bitcast.4), calls=%async_computation.2 | async-start | bytes 65536 | tf_op jit(solution)/shard_map/all_to_all | solution.py:25
  157.4 16.6 %copy-start = (bf16[8,8,1792]{2,1,0:T(8,128)(2,1)S(1)}, bf16[8,8,1792]{2,1,0:T(8,128)(2,1)}, u32[]{:S(2)}) copy-start(bf16[8,8,1792]{2,1,0:T(8,128)(2,1)} %param.9) | copy-start | bytes 688132
  161.5 12.4 %all-to-all-start.3 = ((bf16[8,8,1024]{2,1,0:T(8,128)(2,1)}), bf16[8,8,1024]{2,1,0:T(8,128)(2,1)S(1)}, u32[]{:S(2)}, u32[]{:S(2)}) async-start(bf16[8,8,1024]{2,1,0:T(8,128)(2,1)} %broadcast_in_dim.4), calls=%async_computation.3 | async-start | bytes 262144 | tf_op jit(solution)/shard_map/all_to_all | solution.py:25
Sparse Core Ops, SparseCore 0:
  10.1 69.9 all-gather.6
  82.2 32.4 all-gather.8
  116.8 49.6 all-gather.10

commit v2 on v1

v2 whole, which is shorter than its diff:
```python
import jax
import jax.numpy as jnp
from jax import lax
from jax.sharding import Mesh, PartitionSpec as P

decay_first = 0.9
decay_second = 0.95
bias_first = 1.0 / (1.0 - 0.9**10)
bias_second = 1.0 / (1.0 - 0.95**10)
step_scale = 0.25
epsilon = 1e-08

fine_axes = ("zh", "y", "x", "zl", "core")
fine_sizes = (2, 8, 4, 4, 2)
dp = ("zh", "y", "x")
rest = ("zh", "y")
fsdp = ("zl", "core")


def exchange(block, axes):
    return lax.all_to_all(block, axes, 0, 0, tiled=True)


def copies(block, axes):
    return exchange(jnp.broadcast_to(block[None], (lax.axis_size(axes),) + block.shape), axes)


def contract(left, right, dims):
    return lax.dot_general(left, right, (dims, ((), ())), preferred_element_type=jnp.float32)


def summed(pieces):
    return jnp.sum(pieces.astype(jnp.float32), axis=0)


def shift(block, pairs):
    return lax.ppermute(block, "x", [(i, j) for i, j in enumerate(pairs)])


def after(block, *others):
    return lax.optimization_barrier((block,) + others)[0]


partner = (1, 0, 3, 2)
mirror = (3, 2, 1, 0)
quarters = (0, 3, 1, 2)


def ranks_by_half(moment):
    rows, ranks = moment.shape
    parts = moment.reshape(rows, 2, 8, 4, 16).transpose(0, 3, 2, 1, 4)
    return jnp.concatenate([parts[:, q : q + 1] for q in quarters], axis=1).reshape(rows, ranks)


def ranks_in_order(moment):
    rows, ranks = moment.shape
    parts = moment.reshape(rows, 4, 8, 2, 16)
    parts = [parts[:, quarters.index(q)][:, None] for q in range(4)]
    return jnp.concatenate(parts, axis=1).transpose(0, 3, 2, 1, 4).reshape(rows, ranks)


def gather(block, axes):
    return lax.all_gather(block, axes, axis=0, tiled=True)


def shards(activations, grad_out, projector, weight, moment_one_in, moment_two_in):
    blocks, rows, ff_local = weight.shape
    rank_total = moment_one_in.shape[2]
    tokens, features = activations.shape
    groups = lax.axis_size(fsdp)
    place = lax.axis_index("x")
    low_place = place < 2

    grad_pair = shift(grad_out, partner)
    act_pair = shift(activations, partner)
    own = gather(gather(projector, "zh"), "y")
    other = shift(own, mirror)
    ranks = own.shape[0]

    def project(basis):
        parts = [
            contract(part, basis, ((1,), (1,))).astype(jnp.bfloat16)
            for part in (grad_out, grad_pair)
        ]
        return jnp.concatenate(parts).reshape(groups, -1, ranks)

    near = summed(exchange(project(own), fsdp))
    far = summed(exchange(project(after(other, near)), fsdp))
    pair_own = shift(own, partner)
    pair_other = shift(other, partner)

    owned = jnp.concatenate(
        (jnp.where(low_place, near, far), jnp.where(low_place, far, near)), axis=1
    ).astype(jnp.bfloat16)
    projected = gather(owned, fsdp)

    low = contract(activations, projected[:tokens], ((0,), (0,)))
    low += contract(act_pair, projected[tokens:], ((0,), (0,)))
    low = low.astype(jnp.bfloat16)
    low = summed(exchange(low.reshape(16, -1, 2 * ranks), rest))
    low = exchange(low.reshape(4, rows, 2 * ranks), "x")
    low_grad = jnp.concatenate((low[0] + low[3], low[1] + low[2]), axis=1)

    first_in = ranks_by_half(moment_one_in[0])
    second_in = ranks_by_half(moment_two_in[0])
    moment_one = decay_first * first_in + (1.0 - decay_first) * low_grad
    moment_two = decay_second * second_in + (1.0 - decay_second) * low_grad * low_grad
    direction = (bias_first * moment_one / (jnp.sqrt(bias_second * moment_two) + epsilon)).astype(
        jnp.bfloat16
    )
    direction, pair_other = lax.optimization_barrier((direction, pair_other))
    stacked = copies(direction, fsdp).reshape(blocks * rows, 4, ranks)

    def columns(owners):
        return lax.dynamic_index_in_dim(
            stacked, ((owners & 1) * 2) ^ ((owners >> 1) * 3), 1, keepdims=False
        )

    update = contract(columns(place), own, ((1,), (0,)))
    update += contract(columns(3 - place), other, ((1,), (0,)))
    update += contract(columns(place ^ 1), pair_own, ((1,), (0,)))
    update += contract(columns(place ^ 2), pair_other, ((1,), (0,)))
    updated = (weight.astype(jnp.float32) - step_scale * update.reshape(weight.shape)).astype(
        jnp.bfloat16
    )
    column = gather(updated[None], "zl")
    halves = [
        lax.all_gather(column[:, part * 4 : part * 4 + 4], "core", axis=1) for part in range(2)
    ]
    both = jnp.concatenate(halves, axis=2)
    new_weight = both.transpose(2, 3, 0, 1, 4).reshape(blocks, rows, 8 * ff_local)
    return (
        new_weight,
        ranks_in_order(moment_one)[None],
        ranks_in_order(moment_two)[None],
    )


def solution(mesh):
    fine = Mesh(mesh.devices.reshape(fine_sizes), fine_axes)
    in_specs = (
        P(dp, fsdp),
        P(dp, fsdp),
        P(dp, fsdp),
        P(None, dp, fsdp),
        P(fsdp, dp, None),
        P(fsdp, dp, None),
    )
    out_specs = (P(None, dp, None), P(fsdp, dp, None), P(fsdp, dp, None))
    return jax.shard_map(shards, mesh=fine, in_specs=in_specs, out_specs=out_specs, check_vma=False)
```

time: 210 us -> 208 us (level)
  starting transfers between devices: 20 us -> 37.9 us
  between operations: 13.9 us -> 1.1 us
  waiting for transfers between devices: 54.9 us -> 47 us
  blocking collectives: 104 us -> 99 us
  local copies, waits for them, and re-layouts: 6.65 us -> 10.7 us
    all_gather x3 -> x0, waiting for transfers between devices: 34 us -> none  [gather(): return lax.all_gather(block, axes, axis=0, tiled=True)]
    all_to_all x3 -> x4, waiting for transfers between devices: 19.5 us -> 47 us  [exchange(): return lax.all_to_all(block, axes, 0, 0, tiled=True)]
    ppermute x0 -> x5, starting transfers between devices: none -> 15.2 us  [shift(): return lax.ppermute(block, 'x', [(i, j) for i, j in enumerate(pairs)])]
    all_to_all x3 -> x4, starting transfers between devices: 19.9 us -> 22.7 us  [exchange(): return lax.all_to_all(block, axes, 0, 0, tiled=True)]
    all_to_all x1, blocking collectives: 25.9 us -> 23.5 us  [exchange(): return lax.all_to_all(block, axes, 0, 0, tiled=True)]
    all_gather x4, blocking collectives: 70.8 us -> 68.5 us  [gather(): return lax.all_gather(block, axes, axis=0, tiled=True)]
    dot_general x3 -> x10, matrix products: 9.22 us -> 9.06 us  [contract(): lax.dot_general(left, right, (dims, ((), ())), preferred_element_type=jnp...]
  transfers between devices with their start and end apart: 6 -> 9, of which waited for: 4 -> 4; matrix products, arithmetic and copies ran while one was open for 6% -> 5% of each run, Pallas kernels for 0% -> 0%
where the time goes in v2:
time: 208 us; the launch traced here: 207 us
  blocking collectives  99 us (48%)
  waiting for transfers between devices  47 us (23%)
  starting transfers between devices  37.9 us (18%)
  local copies, waits for them, and re-layouts  10.7 us (5%)
  matrix products  9.06 us (4%)
  other arithmetic  2.24 us (1%)
    all_gather x4, blocking collectives, gather(): return lax.all_gather(block, axes, axis=0, tiled=True)  68.5 us
    all_to_all x4, waiting for transfers between devices, exchange(): return lax.all_to_all(block, axes, 0, 0, tiled=True)  47 us
    all_to_all x1, blocking collectives, exchange(): return lax.all_to_all(block, axes, 0, 0, tiled=True)  23.5 us
    all_to_all x4, starting transfers between devices, exchange(): return lax.all_to_all(block, axes, 0, 0, tiled=True)  22.7 us
    ppermute x5, starting transfers between devices, shift(): return lax.ppermute(block, 'x', [(i, j) for i, j in enumerate(pairs)])  15.2 us
    dot_general x10, matrix products, contract(): lax.dot_general(left, right, (dims, ((), ())), preferred_element_type=jnp...  9.06 us
    all_gather x2, blocking collectives, shards(): lax.all_gather(column[:, part * 4:part * 4 + 4], 'core', axis=1)  7.01 us
  transfers between devices with their start and end apart: 9, of which 4 were waited for; matrix products, arithmetic and copies ran while one was open for 5% of the time, Pallas kernels for 0%

profile of v2, /device:TPU:1, one launch (start us, length us, event | category | flops | bytes accessed | tf_op | source)
XLA Modules:
  0.0 206.9 jit_solution(5159217945243947620)
XLA Ops:
  0.6 4.0 %collective-permute-start = (bf16[384,1792]{1,0:T(8,128)(2,1)}, bf16[384,1792]{1,0:T(8,128)(2,1)S(1)}, u32[]{:S(2)}, u32[]{:S(2)}) collective-permute-start(bf16[384,1792]{1,0:T(8,128)(2,1)} %param.7), channel_id=1, source_target_pairs={{0,8},{8,0},{16,24},{24,16},{1,9},{9,1},{17,25},{25,17},{2,10},{10... | collective-permute-start | bytes 4128776 | tf_op jit(solution)/shard_map/ppermute | solution.py:37
  4.6 11.3 %all_gather.24 = bf16[32,1792]{1,0:T(8,128)(2,1)S(1)} all-gather(bf16[16,1792]{1,0:T(8,128)(2,1)} %param.8), channel_id=1, replica_groups=mesh['zh'=2,'y'=8,'x'=4,'zl'=4,'core'=2] {'zh'}, dimensions={0}, use_global_device_ids=true | all-gather | bytes 172032 | tf_op jit(solution)/shard_map/all_gather | solution.py:63
  15.9 23.0 %all_gather.25 = bf16[256,1792]{1,0:T(8,128)(2,1)S(1)} all-gather(bf16[32,1792]{1,0:T(8,128)(2,1)S(1)} %all_gather.24), channel_id=1, replica_groups=mesh['zh'=2,'y'=8,'x'=4,'zl'=4,'core'=2] {'y'}, dimensions={0}, use_global_device_ids=true | all-gather | bytes 1032192 | tf_op jit(solution)/shard_map/all_gather | solution.py:63
  38.9 3.7 %collective-permute-start.1 = (bf16[256,1792]{1,0:T(8,128)(2,1)S(1)}, bf16[256,1792]{1,0:T(8,128)(2,1)S(1)}, u32[]{:S(2)}, u32[]{:S(2)}) collective-permute-start(bf16[256,1792]{1,0:T(8,128)(2,1)S(1)} %all_gather.25), channel_id=1, source_target_pairs={{0,24},{8,16},{16,8},{24,0},{1,25},{9,17},{17,9},{25,1},{2,26},{10... | collective-permute-start | bytes 2752520 | tf_op jit(solution)/shard_map/ppermute | solution.py:37
  42.6 1.9 convolution_convert_fusion.3
  44.5 0.6 convolution_convert_fusion.2
  45.1 23.5 %all_to_all.25 = bf16[8,96,256]{2,1,0:T(8,128)(2,1)S(1)} all-to-all(bf16[8,96,256]{2,1,0:T(8,128)(2,1)S(1)} %bitcast.58), channel_id=1, replica_groups=mesh['zh'=2,'y'=8,'x'=4,'zl'=4,'core'=2] {'zl','core'}, dimensions={0} | all-to-all | bytes 786432 | tf_op jit(solution)/shard_map/all_to_all | solution.py:21
  68.7 0.7 fusion.5
  69.3 0.7 fusion.6
  70.1 0.9 copy.17
  71.0 4.2 %all-to-all-start.1 = ((bf16[8,96,256]{2,1,0:T(8,128)(2,1)}), bf16[8,96,256]{2,1,0:T(8,128)(2,1)S(1)}, u32[]{:S(2)}, u32[]{:S(2)}) async-start(bf16[8,96,256]{2,1,0:T(8,128)(2,1)} %bitcast.4), calls=%async_computation.1 | async-start | bytes 786432 | tf_op jit(solution)/shard_map/all_to_all | solution.py:21
  75.2 2.2 %collective-permute-start.2 = (bf16[384,512]{1,0:T(8,128)(2,1)S(1)}, bf16[384,512]{1,0:T(8,128)(2,1)S(1)}, u32[]{:S(2)}, u32[]{:S(2)}) collective-permute-start(bf16[384,512]{1,0:T(8,128)(2,1)S(1)} %copy-done), channel_id=1, source_target_pairs={{0,8},{8,0},{16,24},{24,16},{1,9},{9,1},{17,25},{25,17},{2,10},{10... | collective-permute-start | bytes 1179656 | tf_op jit(solution)/shard_map/ppermute | solution.py:37
  77.4 9.5 %all-to-all-done.1 = bf16[8,96,256]{2,1,0:T(8,128)(2,1)S(1)} async-done(((bf16[8,96,256]{2,1,0:T(8,128)(2,1)}), bf16[8,96,256]{2,1,0:T(8,128)(2,1)S(1)}, u32[]{:S(2)}, u32[]{:S(2)}) %all-to-all-start.1) | async-done | bytes 393248 | tf_op jit(solution)/shard_map/all_to_all | solution.py:21
  87.0 16.4 %all_gather.26 = bf16[768,512]{1,0:T(8,128)(2,1)S(1)} all-gather(bf16[96,512]{1,0:T(8,128)(2,1)S(1)} %pad_maximum_fusion.3), channel_id=1, replica_groups=mesh['zh'=2,'y'=8,'x'=4,'zl'=4,'core'=2] {'zl','core'}, dimensions={0}, use_global_device_ids=true | all-gather | bytes 884736 | tf_op jit(solution)/shard_map/all_gather | solution.py:63
  103.4 0.5 fusion.8
  103.9 1.3 fusion.4
  105.2 10.3 %all-to-all-start.2 = ((bf16[16,32,512]{2,1,0:T(8,128)(2,1)}), bf16[16,32,512]{2,1,0:T(8,128)(2,1)S(1)}, u32[]{:S(2)}, u32[]{:S(2)}) async-start(bf16[16,32,512]{2,1,0:T(8,128)(2,1)} %bitcast.6), calls=%async_computation.2 | async-start | bytes 1048576 | tf_op jit(solution)/shard_map/all_to_all | solution.py:21
  115.5 2.2 %collective-permute-start.4 = (bf16[256,1792]{1,0:T(8,128)(2,1)S(1)}, bf16[256,1792]{1,0:T(8,128)(2,1)}, u32[]{:S(2)}, u32[]{:S(2)}) collective-permute-start(bf16[256,1792]{1,0:T(8,128)(2,1)S(1)} %all_gather.25), channel_id=1, source_target_pairs={{0,8},{8,0},{16,24},{24,16},{1,9},{9,1},{17,25},{25,17},{2,10},{10... | collective-permute-start | bytes 2752520 | tf_op jit(solution)/shard_map/ppermute | solution.py:37
  117.8 0.2 reshape_squeeze.6
  118.0 0.2 reshape_squeeze.7
  118.4 3.1 %collective-permute-start.3 = (bf16[256,1792]{1,0:T(8,128)(2,1)S(1)}, bf16[256,1792]{1,0:T(8,128)(2,1)}, u32[]{:S(2)}, u32[]{:S(2)}) collective-permute-start(bf16[256,1792]{1,0:T(8,128)(2,1)S(1)} %collective-permute-done.1), channel_id=1, source_target_pairs={{0,8},{8,0},{16,24},{24,16},{1,9},{9,1},{17,25},{25,17},{2,10},{10... | collective-permute-start | bytes 2752520 | tf_op jit(solution)/shard_map/ppermute | solution.py:37
  121.4 11.8 %all-to-all-done.2 = bf16[16,32,512]{2,1,0:T(8,128)(2,1)S(1)} async-done(((bf16[16,32,512]{2,1,0:T(8,128)(2,1)}), bf16[16,32,512]{2,1,0:T(8,128)(2,1)S(1)}, u32[]{:S(2)}, u32[]{:S(2)}) %all-to-all-start.2) | async-done | bytes 524320 | tf_op jit(solution)/shard_map/all_to_all | solution.py:21
  133.2 0.7 convert_reduce_fusion
  133.9 3.3 %all-to-all-start.3 = ((f32[4,8,512]{2,1,0:T(8,128)}), f32[4,8,512]{2,1,0:T(8,128)S(1)}, u32[]{:S(2)}, u32[]{:S(2)}) async-start(f32[4,8,512]{2,1,0:T(8,128)} %bitcast.7), calls=%async_computation.3 | async-start | bytes 131072 | tf_op jit(solution)/shard_map/all_to_all | solution.py:21
  137.5 22.0 %all-to-all-done.3 = f32[4,8,512]{2,1,0:T(8,128)S(1)} async-done(((f32[4,8,512]{2,1,0:T(8,128)}), f32[4,8,512]{2,1,0:T(8,128)S(1)}, u32[]{:S(2)}, u32[]{:S(2)}) %all-to-all-start.3) | async-done | bytes 65568 | tf_op jit(solution)/shard_map/all_to_all | solution.py:21
  159.6 0.2 add.80
  159.9 0.2 add.81
  160.2 0.7 fusion.10
  160.9 0.2 copy.18
  161.1 0.3 mul.102
  161.6 0.3 mul.95
  162.4 0.7 broadcast_in_dim.4
  163.0 4.9 %all-to-all-start.4 = ((bf16[8,8,1024]{2,1,0:T(8,128)(2,1)}), bf16[8,8,1024]{2,1,0:T(8,128)(2,1)S(1)}, u32[]{:S(2)}, u32[]{:S(2)}) async-start(bf16[8,8,1024]{2,1,0:T(8,128)(2,1)} %broadcast_in_dim.4), calls=%async_computation.4 | async-start | bytes 262144 | tf_op jit(solution)/shard_map/all_to_all | solution.py:21
  167.9 0.2 maximum_bitcast_fusion.2
  168.1 0.9 broadcast_in_dim_reshape.7
  169.0 0.2 maximum_bitcast_fusion.1
  169.2 0.9 broadcast_in_dim_reshape.6
  170.1 3.7 %all-to-all-done.4 = bf16[8,8,1024]{2,1,0:T(8,128)(2,1)S(1)} async-done(((bf16[8,8,1024]{2,1,0:T(8,128)(2,1)}), bf16[8,8,1024]{2,1,0:T(8,128)(2,1)S(1)}, u32[]{:S(2)}, u32[]{:S(2)}) %all-to-all-start.4) | async-done | bytes 131104 | tf_op jit(solution)/shard_map/all_to_all | solution.py:21
  173.8 0.3 constant_dynamic-slice_fusion
  174.1 0.3 fusion.22
  174.4 0.3 convolution_add_fusion.2
  174.7 1.5 convolution_add_fusion.1
  176.2 1.5 fusion.3
  177.7 17.8 %all-gather = bf16[32,8,1792]{2,1,0:T(8,128)(2,1)S(1)} all-gather(bf16[8,8,1792]{2,1,0:T(8,128)(2,1)S(1)} %fusion.3), channel_id=2, replica_groups=mesh['zh'=2,'y'=8,'x'=4,'zl'=4,'core'=2] {'zl'}, dimensions={0}, use_global_device_ids=true | all-gather | bytes 1146880 | tf_op jit(solution)/shard_map/all_gather | solution.py:63
  195.5 4.4 %all-gather.1 = bf16[4,8,8,1792]{3,2,1,0:T(8,128)(2,1)S(1)} all-gather(bf16[4,4,8,1792]{3,2,1,0:T(8,128)(2,1)S(1)} %get-tuple-element.9), channel_id=3, replica_groups=mesh['zh'=2,'y'=8,'x'=4,'zl'=4,'core'=2] {'core'}, dimensions={1}, use_global_device_ids=true | all-gather | bytes 1376256 | tf_op jit(solution)/shard_map/all_gather | solution.py:128
  199.9 2.6 %all-gather.2 = bf16[4,8,8,1792]{3,2,1,0:T(8,128)(2,1)S(1)} all-gather(bf16[4,4,8,1792]{3,2,1,0:T(8,128)(2,1)S(1)} %get-tuple-element.10), channel_id=4, replica_groups=mesh['zh'=2,'y'=8,'x'=4,'zl'=4,'core'=2] {'core'}, dimensions={1}, use_global_device_ids=true | all-gather | bytes 1376256 | tf_op jit(solution)/shard_map/all_gather | solution.py:128
  202.7 1.9 copy.19
  204.6 2.3 %reshape.53 = bf16[8,8,14336]{2,1,0:T(8,128)(2,1)} reshape(bf16[8,8,4,2,1792]{4,3,2,1,0:T(2,128)(2,1)S(1)} %copy.19) | data formatting | bytes 3670016 | tf_op jit(solution)/shard_map/reshape | solution.py:131
  (36 shorter events, 1.6 us)
Async XLA Ops:
  0.6 43.9 %collective-permute-start = (bf16[384,1792]{1,0:T(8,128)(2,1)}, bf16[384,1792]{1,0:T(8,128)(2,1)S(1)}, u32[]{:S(2)}, u32[]{:S(2)}) collective-permute-start(bf16[384,1792]{1,0:T(8,128)(2,1)} %param.7), channel_id=1, source_target_pairs={{0,8},{8,0},{16,24},{24,16},{1,9},{9,1},{17,25},{25,17},{2,10},{10... | collective-permute-start | bytes 4128776 | tf_op jit(solution)/shard_map/ppermute | solution.py:37
  38.9 29.8 %collective-permute-start.1 = (bf16[256,1792]{1,0:T(8,128)(2,1)S(1)}, bf16[256,1792]{1,0:T(8,128)(2,1)S(1)}, u32[]{:S(2)}, u32[]{:S(2)}) collective-permute-start(bf16[256,1792]{1,0:T(8,128)(2,1)S(1)} %all_gather.25), channel_id=1, source_target_pairs={{0,24},{8,16},{16,8},{24,0},{1,25},{9,17},{17,9},{25,1},{2,26},{10... | collective-permute-start | bytes 2752520 | tf_op jit(solution)/shard_map/ppermute | solution.py:37
  45.1 23.6 %copy-start.4 = (bf16[384,1792]{1,0:T(8,128)(2,1)S(1)}, bf16[384,1792]{1,0:T(8,128)(2,1)}, u32[]{:S(2)}) copy-start(bf16[384,1792]{1,0:T(8,128)(2,1)} %param.7) | copy-start | bytes 4128772
  70.0 5.2 %copy-start = (bf16[384,512]{1,0:T(8,128)(2,1)S(1)}, bf16[384,512]{1,0:T(8,128)(2,1)}, u32[]{:S(2)}) copy-start(bf16[384,512]{1,0:T(8,128)(2,1)} %param.6) | copy-start | bytes 1179652
  71.0 15.9 %all-to-all-start.1 = ((bf16[8,96,256]{2,1,0:T(8,128)(2,1)}), bf16[8,96,256]{2,1,0:T(8,128)(2,1)S(1)}, u32[]{:S(2)}, u32[]{:S(2)}) async-start(bf16[8,96,256]{2,1,0:T(8,128)(2,1)} %bitcast.4), calls=%async_computation.1 | async-start | bytes 786432 | tf_op jit(solution)/shard_map/all_to_all | solution.py:21
  75.2 28.7 %collective-permute-start.2 = (bf16[384,512]{1,0:T(8,128)(2,1)S(1)}, bf16[384,512]{1,0:T(8,128)(2,1)S(1)}, u32[]{:S(2)}, u32[]{:S(2)}) collective-permute-start(bf16[384,512]{1,0:T(8,128)(2,1)S(1)} %copy-done), channel_id=1, source_target_pairs={{0,8},{8,0},{16,24},{24,16},{1,9},{9,1},{17,25},{25,17},{2,10},{10... | collective-permute-start | bytes 1179656 | tf_op jit(solution)/shard_map/ppermute | solution.py:37
  103.9 13.9 %copy-start.2 = (f32[1,8,1024]{2,1,0:T(8,128)S(1)}, f32[1,8,1024]{2,1,0:T(8,128)}, u32[]{:S(2)}) copy-start(f32[1,8,1024]{2,1,0:T(8,128)} %param.10) | copy-start | bytes 98308
  103.9 14.1 %copy-start.3 = (f32[1,8,1024]{2,1,0:T(8,128)S(1)}, f32[1,8,1024]{2,1,0:T(8,128)}, u32[]{:S(2)}) copy-start(f32[1,8,1024]{2,1,0:T(8,128)} %param.11) | copy-start | bytes 98308
  105.2 28.0 %all-to-all-start.2 = ((bf16[16,32,512]{2,1,0:T(8,128)(2,1)}), bf16[16,32,512]{2,1,0:T(8,128)(2,1)S(1)}, u32[]{:S(2)}, u32[]{:S(2)}) async-start(bf16[16,32,512]{2,1,0:T(8,128)(2,1)} %bitcast.6), calls=%async_computation.2 | async-start | bytes 1048576 | tf_op jit(solution)/shard_map/all_to_all | solution.py:21
  115.5 59.2 %collective-permute-start.4 = (bf16[256,1792]{1,0:T(8,128)(2,1)S(1)}, bf16[256,1792]{1,0:T(8,128)(2,1)}, u32[]{:S(2)}, u32[]{:S(2)}) collective-permute-start(bf16[256,1792]{1,0:T(8,128)(2,1)S(1)} %all_gather.25), channel_id=1, source_target_pairs={{0,8},{8,0},{16,24},{24,16},{1,9},{9,1},{17,25},{25,17},{2,10},{10... | collective-permute-start | bytes 2752520 | tf_op jit(solution)/shard_map/ppermute | solution.py:37
  118.4 44.0 %collective-permute-start.3 = (bf16[256,1792]{1,0:T(8,128)(2,1)S(1)}, bf16[256,1792]{1,0:T(8,128)(2,1)}, u32[]{:S(2)}, u32[]{:S(2)}) collective-permute-start(bf16[256,1792]{1,0:T(8,128)(2,1)S(1)} %collective-permute-done.1), channel_id=1, source_target_pairs={{0,8},{8,0},{16,24},{24,16},{1,9},{9,1},{17,25},{25,17},{2,10},{10... | collective-permute-start | bytes 2752520 | tf_op jit(solution)/shard_map/ppermute | solution.py:37
  133.9 25.6 %all-to-all-start.3 = ((f32[4,8,512]{2,1,0:T(8,128)}), f32[4,8,512]{2,1,0:T(8,128)S(1)}, u32[]{:S(2)}, u32[]{:S(2)}) async-start(f32[4,8,512]{2,1,0:T(8,128)} %bitcast.7), calls=%async_computation.3 | async-start | bytes 131072 | tf_op jit(solution)/shard_map/all_to_all | solution.py:21
  163.0 10.7 %all-to-all-start.4 = ((bf16[8,8,1024]{2,1,0:T(8,128)(2,1)}), bf16[8,8,1024]{2,1,0:T(8,128)(2,1)S(1)}, u32[]{:S(2)}, u32[]{:S(2)}) async-start(bf16[8,8,1024]{2,1,0:T(8,128)(2,1)} %broadcast_in_dim.4), calls=%async_computation.4 | async-start | bytes 262144 | tf_op jit(solution)/shard_map/all_to_all | solution.py:21
  174.7 1.5 copy-start.1

commit v3 on v2

--- a/solution.py
+++ b/solution.py
@@ -85,6 +85,7 @@
         return jnp.concatenate(parts).reshape(groups, -1, ranks)
 
     near = summed(exchange(project(own), fsdp))
+    near, act_pair = lax.optimization_barrier((near, act_pair))
     far = summed(exchange(project(after(other, near)), fsdp))
     pair_own = shift(own, partner)
     pair_other = shift(other, partner)
@@ -92,7 +93,7 @@
     owned = jnp.concatenate(
         (jnp.where(low_place, near, far), jnp.where(low_place, far, near)), axis=1
     ).astype(jnp.bfloat16)
-    projected = gather(owned, fsdp)
+    projected = after(gather(owned, fsdp), pair_own)
 
     low = contract(activations, projected[:tokens], ((0,), (0,)))
     low += contract(act_pair, projected[tokens:], ((0,), (0,)))
@@ -108,7 +109,6 @@
     direction = (bias_first * moment_one / (jnp.sqrt(bias_second * moment_two) + epsilon)).astype(
         jnp.bfloat16
     )
-    direction, pair_other = lax.optimization_barrier((direction, pair_other))
     stacked = copies(direction, fsdp).reshape(blocks * rows, 4, ranks)
 
     def columns(owners):
@@ -127,8 +127,8 @@
     halves = [
         lax.all_gather(column[:, part * 4 : part * 4 + 4], "core", axis=1) for part in range(2)
     ]
-    both = jnp.concatenate(halves, axis=2)
-    new_weight = both.transpose(2, 3, 0, 1, 4).reshape(blocks, rows, 8 * ff_local)
+    both = jnp.concatenate(halves, axis=2).reshape(8, blocks, rows, ff_local)
+    new_weight = both.transpose(1, 2, 0, 3).reshape(blocks, rows, 8 * ff_local)
     return (
         new_weight,
         ranks_in_order(moment_one)[None],

time: 208 us -> 194 us (0.933)
  blocking collectives: 99 us -> 75.9 us
  starting transfers between devices: 37.9 us -> 53.8 us
  waiting for transfers between devices: 47 us -> 41.4 us
  local copies, waits for them, and re-layouts: 10.7 us -> 7.92 us
    all_to_all x1 -> x0, blocking collectives: 23.5 us -> none  [exchange(): return lax.all_to_all(block, axes, 0, 0, tiled=True)]
    all_to_all x4 -> x5, starting transfers between devices: 22.7 us -> 38.4 us  [exchange(): return lax.all_to_all(block, axes, 0, 0, tiled=True)]
    all_to_all x4 -> x5, waiting for transfers between devices: 47 us -> 40.5 us  [exchange(): return lax.all_to_all(block, axes, 0, 0, tiled=True)]
    reshape x1 -> x0, local copies, waits for them, and re-layouts: 2.31 us -> none  [shards(): both.transpose(2, 3, 0, 1, 4).reshape(blocks, rows, 8 * ff_local)]
  transfers between devices with their start and end apart: 9 -> 10, of which waited for: 4 -> 6; matrix products, arithmetic and copies ran while one was open for 5% -> 6% of each run, Pallas kernels for 0% -> 0%
where the time goes in v3:
time: 194 us; the launch traced here: 193 us
  blocking collectives  75.9 us (39%)
  starting transfers between devices  53.8 us (28%)
  waiting for transfers between devices  41.4 us (21%)
  matrix products  10.4 us (5%)
  local copies, waits for them, and re-layouts  7.92 us (4%)
  other arithmetic  2.99 us (2%)
    all_gather x4, blocking collectives, gather(): return lax.all_gather(block, axes, axis=0, tiled=True)  67.9 us
    all_to_all x5, waiting for transfers between devices, exchange(): return lax.all_to_all(block, axes, 0, 0, tiled=True)  40.5 us
    all_to_all x5, starting transfers between devices, exchange(): return lax.all_to_all(block, axes, 0, 0, tiled=True)  38.4 us
    ppermute x5, starting transfers between devices, shift(): return lax.ppermute(block, 'x', [(i, j) for i, j in enumerate(pairs)])  15.4 us
    dot_general x10, matrix products, contract(): lax.dot_general(left, right, (dims, ((), ())), preferred_element_type=jnp...  10.4 us
    all_gather x2, blocking collectives, shards(): lax.all_gather(column[:, part * 4:part * 4 + 4], 'core', axis=1)  7.98 us
  transfers between devices with their start and end apart: 10, of which 6 were waited for; matrix products, arithmetic and copies ran while one was open for 6% of the time, Pallas kernels for 0%

profile of v3, /device:TPU:1, one launch (start us, length us, event | category | flops | bytes accessed | tf_op | source)
XLA Modules:
  0.0 193.4 jit_solution(17467476857167934754)
XLA Ops:
  0.6 4.0 %collective-permute-start = (bf16[384,1792]{1,0:T(8,128)(2,1)}, bf16[384,1792]{1,0:T(8,128)(2,1)S(1)}, u32[]{:S(2)}, u32[]{:S(2)}) collective-permute-start(bf16[384,1792]{1,0:T(8,128)(2,1)} %param.7), channel_id=1, source_target_pairs={{0,8},{8,0},{16,24},{24,16},{1,9},{9,1},{17,25},{25,17},{2,10},{10... | collective-permute-start | bytes 4128776 | tf_op jit(solution)/shard_map/ppermute | solution.py:37
  4.6 11.3 %all_gather.24 = bf16[32,1792]{1,0:T(8,128)(2,1)S(1)} all-gather(bf16[16,1792]{1,0:T(8,128)(2,1)} %param.8), channel_id=1, replica_groups=mesh['zh'=2,'y'=8,'x'=4,'zl'=4,'core'=2] {'zh'}, dimensions={0}, use_global_device_ids=true | all-gather | bytes 172032 | tf_op jit(solution)/shard_map/all_gather | solution.py:63
  15.9 23.0 %all_gather.25 = bf16[256,1792]{1,0:T(8,128)(2,1)S(1)} all-gather(bf16[32,1792]{1,0:T(8,128)(2,1)S(1)} %all_gather.24), channel_id=1, replica_groups=mesh['zh'=2,'y'=8,'x'=4,'zl'=4,'core'=2] {'y'}, dimensions={0}, use_global_device_ids=true | all-gather | bytes 1032192 | tf_op jit(solution)/shard_map/all_gather | solution.py:63
  38.9 3.7 %collective-permute-start.2 = (bf16[256,1792]{1,0:T(8,128)(2,1)S(1)}, bf16[256,1792]{1,0:T(8,128)(2,1)S(1)}, u32[]{:S(2)}, u32[]{:S(2)}) collective-permute-start(bf16[256,1792]{1,0:T(8,128)(2,1)S(1)} %all_gather.25), channel_id=1, source_target_pairs={{0,24},{8,16},{16,8},{24,0},{1,25},{9,17},{17,9},{25,1},{2,26},{10... | collective-permute-start | bytes 2752520 | tf_op jit(solution)/shard_map/ppermute | solution.py:37
  42.6 1.9 convolution_convert_fusion.3
  44.5 0.6 convolution_convert_fusion.2
  45.1 0.8 pad_maximum_fusion.1
  45.9 11.9 %all-to-all-start = ((bf16[8,96,256]{2,1,0:T(8,128)(2,1)}), bf16[8,96,256]{2,1,0:T(8,128)(2,1)S(1)}, u32[]{:S(2)}, u32[]{:S(2)}) async-start(bf16[8,96,256]{2,1,0:T(8,128)(2,1)} %bitcast.1), calls=%async_computation | async-start | bytes 786432 | tf_op jit(solution)/shard_map/all_to_all | solution.py:21
  57.7 2.2 %collective-permute-start.1 = (bf16[384,512]{1,0:T(8,128)(2,1)S(1)}, bf16[384,512]{1,0:T(8,128)(2,1)S(1)}, u32[]{:S(2)}, u32[]{:S(2)}) collective-permute-start(bf16[384,512]{1,0:T(8,128)(2,1)S(1)} %copy-done), channel_id=1, source_target_pairs={{0,8},{8,0},{16,24},{24,16},{1,9},{9,1},{17,25},{25,17},{2,10},{10... | collective-permute-start | bytes 1179656 | tf_op jit(solution)/shard_map/ppermute | solution.py:37
  60.0 9.5 %all-to-all-done = bf16[8,96,256]{2,1,0:T(8,128)(2,1)S(1)} async-done(((bf16[8,96,256]{2,1,0:T(8,128)(2,1)}), bf16[8,96,256]{2,1,0:T(8,128)(2,1)S(1)}, u32[]{:S(2)}, u32[]{:S(2)}) %all-to-all-start) | async-done | bytes 393248 | tf_op jit(solution)/shard_map/all_to_all | solution.py:21
  69.5 0.9 collective-permute-done.1
  70.4 2.0 %fusion.5 = bf16[384,256]{0,1:T(8,128)(2,1)S(1)} fusion(bf16[256,1792]{1,0:T(8,128)(2,1)S(1)} %collective-permute-done.2, bf16[384,1792]{1,0:T(8,128)(2,1)} %param.7), kind=kOutput, calls=%fused_computation.15 | convolution fusion | flops 352419840 | bytes 2490368 | tf_op jit(solution)/shard_map/dot_general | solution.py:29
  72.4 0.7 fusion.6
  73.1 0.9 copy.22
  74.0 5.5 %all-to-all-start.1 = ((bf16[8,96,256]{2,1,0:T(8,128)(2,1)}), bf16[8,96,256]{2,1,0:T(8,128)(2,1)S(1)}, u32[]{:S(2)}, u32[]{:S(2)}) async-start(bf16[8,96,256]{2,1,0:T(8,128)(2,1)} %bitcast.4), calls=%async_computation.1 | async-start | bytes 786432 | tf_op jit(solution)/shard_map/all_to_all | solution.py:21
  79.5 2.2 %collective-permute-start.3 = (bf16[256,1792]{1,0:T(8,128)(2,1)S(1)}, bf16[256,1792]{1,0:T(8,128)(2,1)}, u32[]{:S(2)}, u32[]{:S(2)}) collective-permute-start(bf16[256,1792]{1,0:T(8,128)(2,1)S(1)} %all_gather.25), channel_id=1, source_target_pairs={{0,8},{8,0},{16,24},{24,16},{1,9},{9,1},{17,25},{25,17},{2,10},{10... | collective-permute-start | bytes 2752520 | tf_op jit(solution)/shard_map/ppermute | solution.py:37
  81.7 9.5 %all-to-all-done.1 = bf16[8,96,256]{2,1,0:T(8,128)(2,1)S(1)} async-done(((bf16[8,96,256]{2,1,0:T(8,128)(2,1)}), bf16[8,96,256]{2,1,0:T(8,128)(2,1)S(1)}, u32[]{:S(2)}, u32[]{:S(2)}) %all-to-all-start.1) | async-done | bytes 393248 | tf_op jit(solution)/shard_map/all_to_all | solution.py:21
  91.3 16.4 %all_gather.26 = bf16[768,512]{1,0:T(8,128)(2,1)S(1)} all-gather(bf16[96,512]{1,0:T(8,128)(2,1)S(1)} %pad_maximum_fusion.4), channel_id=1, replica_groups=mesh['zh'=2,'y'=8,'x'=4,'zl'=4,'core'=2] {'zl','core'}, dimensions={0}, use_global_device_ids=true | all-gather | bytes 884736 | tf_op jit(solution)/shard_map/all_gather | solution.py:63
  107.7 0.5 convolution_bitcast_fusion
  108.2 1.2 fusion.4
  109.5 10.3 %all-to-all-start.2 = ((bf16[16,32,512]{2,1,0:T(8,128)(2,1)}), bf16[16,32,512]{2,1,0:T(8,128)(2,1)S(1)}, u32[]{:S(2)}, u32[]{:S(2)}) async-start(bf16[16,32,512]{2,1,0:T(8,128)(2,1)} %bitcast.6), calls=%async_computation.2 | async-start | bytes 1048576 | tf_op jit(solution)/shard_map/all_to_all | solution.py:21
  119.8 0.2 reshape_squeeze.6
  120.1 0.2 reshape_squeeze.7
  120.4 17.1 %all-to-all-done.2 = bf16[16,32,512]{2,1,0:T(8,128)(2,1)S(1)} async-done(((bf16[16,32,512]{2,1,0:T(8,128)(2,1)}), bf16[16,32,512]{2,1,0:T(8,128)(2,1)S(1)}, u32[]{:S(2)}, u32[]{:S(2)}) %all-to-all-start.2) | async-done | bytes 524320 | tf_op jit(solution)/shard_map/all_to_all | solution.py:21
  137.5 0.7 convert_reduce_fusion
  138.2 3.3 %all-to-all-start.3 = ((f32[4,8,512]{2,1,0:T(8,128)}), f32[4,8,512]{2,1,0:T(8,128)S(1)}, u32[]{:S(2)}, u32[]{:S(2)}) async-start(f32[4,8,512]{2,1,0:T(8,128)} %bitcast.7), calls=%async_computation.3 | async-start | bytes 131072 | tf_op jit(solution)/shard_map/all_to_all | solution.py:21
  141.8 3.3 %collective-permute-start.4 = (bf16[256,1792]{1,0:T(8,128)(2,1)S(1)}, bf16[256,1792]{1,0:T(8,128)(2,1)}, u32[]{:S(2)}, u32[]{:S(2)}) collective-permute-start(bf16[256,1792]{1,0:T(8,128)(2,1)S(1)} %collective-permute-done.2), channel_id=1, source_target_pairs={{0,8},{8,0},{16,24},{24,16},{1,9},{9,1},{17,25},{25,17},{2,10},{10... | collective-permute-start | bytes 2752520 | tf_op jit(solution)/shard_map/ppermute | solution.py:37
  145.1 0.8 all-to-all-done.3
  145.9 0.2 add.85
  146.5 0.7 fusion.9
  147.8 0.3 mul.123
  148.4 0.3 mul.130
  148.7 0.7 broadcast_in_dim.4
  149.4 7.4 %all-to-all-start.4 = ((bf16[8,8,1024]{2,1,0:T(8,128)(2,1)}), bf16[8,8,1024]{2,1,0:T(8,128)(2,1)S(1)}, u32[]{:S(2)}, u32[]{:S(2)}) async-start(bf16[8,8,1024]{2,1,0:T(8,128)(2,1)} %broadcast_in_dim.4), calls=%async_computation.4 | async-start | bytes 262144 | tf_op jit(solution)/shard_map/all_to_all | solution.py:21
  156.8 0.2 maximum_bitcast_fusion.1
  157.0 0.9 broadcast_in_dim_reshape.7
  157.9 0.2 maximum_bitcast_fusion
  158.1 0.9 broadcast_in_dim_reshape.6
  159.0 3.7 %all-to-all-done.4 = bf16[8,8,1024]{2,1,0:T(8,128)(2,1)S(1)} async-done(((bf16[8,8,1024]{2,1,0:T(8,128)(2,1)}), bf16[8,8,1024]{2,1,0:T(8,128)(2,1)S(1)}, u32[]{:S(2)}, u32[]{:S(2)}) %all-to-all-start.4) | async-done | bytes 131104 | tf_op jit(solution)/shard_map/all_to_all | solution.py:21
  162.7 0.3 constant_dynamic-slice_fusion
  163.0 0.3 fusion.21
  163.3 0.3 convolution_add_fusion.2
  163.6 1.5 convolution_add_fusion.1
  165.1 1.5 fusion.3
  166.6 17.2 %all-gather = bf16[32,8,1792]{2,1,0:T(8,128)(2,1)S(1)} all-gather(bf16[8,8,1792]{2,1,0:T(8,128)(2,1)S(1)} %fusion.3), channel_id=2, replica_groups=mesh['zh'=2,'y'=8,'x'=4,'zl'=4,'core'=2] {'zl'}, dimensions={0}, use_global_device_ids=true | all-gather | bytes 1146880 | tf_op jit(solution)/shard_map/all_gather | solution.py:63
  183.9 5.5 %all-gather.1 = bf16[4,8,8,1792]{3,2,1,0:T(8,128)(2,1)S(1)} all-gather(bf16[4,4,8,1792]{3,2,1,0:T(8,128)(2,1)S(1)} %get-tuple-element.11), channel_id=3, replica_groups=mesh['zh'=2,'y'=8,'x'=4,'zl'=4,'core'=2] {'core'}, dimensions={1}, use_global_device_ids=true | all-gather | bytes 1376256 | tf_op jit(solution)/shard_map/all_gather | solution.py:128
  189.4 2.5 %all-gather.2 = bf16[4,8,8,1792]{3,2,1,0:T(8,128)(2,1)S(1)} all-gather(bf16[4,4,8,1792]{3,2,1,0:T(8,128)(2,1)S(1)} %get-tuple-element.12), channel_id=4, replica_groups=mesh['zh'=2,'y'=8,'x'=4,'zl'=4,'core'=2] {'core'}, dimensions={1}, use_global_device_ids=true | all-gather | bytes 1376256 | tf_op jit(solution)/shard_map/all_gather | solution.py:128
  192.0 1.4 copy.24
  (38 shorter events, 2.0 us)
Async XLA Ops:
  0.6 43.9 %collective-permute-start = (bf16[384,1792]{1,0:T(8,128)(2,1)}, bf16[384,1792]{1,0:T(8,128)(2,1)S(1)}, u32[]{:S(2)}, u32[]{:S(2)}) collective-permute-start(bf16[384,1792]{1,0:T(8,128)(2,1)} %param.7), channel_id=1, source_target_pairs={{0,8},{8,0},{16,24},{24,16},{1,9},{9,1},{17,25},{25,17},{2,10},{10... | collective-permute-start | bytes 4128776 | tf_op jit(solution)/shard_map/ppermute | solution.py:37
  38.9 31.5 %collective-permute-start.2 = (bf16[256,1792]{1,0:T(8,128)(2,1)S(1)}, bf16[256,1792]{1,0:T(8,128)(2,1)S(1)}, u32[]{:S(2)}, u32[]{:S(2)}) collective-permute-start(bf16[256,1792]{1,0:T(8,128)(2,1)S(1)} %all_gather.25), channel_id=1, source_target_pairs={{0,24},{8,16},{16,8},{24,0},{1,25},{9,17},{17,9},{25,1},{2,26},{10... | collective-permute-start | bytes 2752520 | tf_op jit(solution)/shard_map/ppermute | solution.py:37
  44.5 1.4 copy-start.4
  45.1 12.7 %copy-start = (bf16[384,512]{1,0:T(8,128)(2,1)S(1)}, bf16[384,512]{1,0:T(8,128)(2,1)}, u32[]{:S(2)}) copy-start(bf16[384,512]{1,0:T(8,128)(2,1)} %param.6) | copy-start | bytes 1179652
  45.9 23.6 %all-to-all-start = ((bf16[8,96,256]{2,1,0:T(8,128)(2,1)}), bf16[8,96,256]{2,1,0:T(8,128)(2,1)S(1)}, u32[]{:S(2)}, u32[]{:S(2)}) async-start(bf16[8,96,256]{2,1,0:T(8,128)(2,1)} %bitcast.1), calls=%async_computation | async-start | bytes 786432 | tf_op jit(solution)/shard_map/all_to_all | solution.py:21
  57.7 12.6 %collective-permute-start.1 = (bf16[384,512]{1,0:T(8,128)(2,1)S(1)}, bf16[384,512]{1,0:T(8,128)(2,1)S(1)}, u32[]{:S(2)}, u32[]{:S(2)}) collective-permute-start(bf16[384,512]{1,0:T(8,128)(2,1)S(1)} %copy-done), channel_id=1, source_target_pairs={{0,8},{8,0},{16,24},{24,16},{1,9},{9,1},{17,25},{25,17},{2,10},{10... | collective-permute-start | bytes 1179656 | tf_op jit(solution)/shard_map/ppermute | solution.py:37
  69.5 2.9 %copy-start.5 = (bf16[384,1792]{1,0:T(8,128)(2,1)S(1)}, bf16[384,1792]{1,0:T(8,128)(2,1)}, u32[]{:S(2)}) copy-start(bf16[384,1792]{1,0:T(8,128)(2,1)} %copy-done.4) | copy-start | bytes 4128772
  74.0 17.2 %all-to-all-start.1 = ((bf16[8,96,256]{2,1,0:T(8,128)(2,1)}), bf16[8,96,256]{2,1,0:T(8,128)(2,1)S(1)}, u32[]{:S(2)}, u32[]{:S(2)}) async-start(bf16[8,96,256]{2,1,0:T(8,128)(2,1)} %bitcast.4), calls=%async_computation.1 | async-start | bytes 786432 | tf_op jit(solution)/shard_map/all_to_all | solution.py:21
  79.5 28.2 %collective-permute-start.3 = (bf16[256,1792]{1,0:T(8,128)(2,1)S(1)}, bf16[256,1792]{1,0:T(8,128)(2,1)}, u32[]{:S(2)}, u32[]{:S(2)}) collective-permute-start(bf16[256,1792]{1,0:T(8,128)(2,1)S(1)} %all_gather.25), channel_id=1, source_target_pairs={{0,8},{8,0},{16,24},{24,16},{1,9},{9,1},{17,25},{25,17},{2,10},{10... | collective-permute-start | bytes 2752520 | tf_op jit(solution)/shard_map/ppermute | solution.py:37
  108.2 11.6 %copy-start.2 = (f32[1,8,1024]{2,1,0:T(8,128)S(1)}, f32[1,8,1024]{2,1,0:T(8,128)}, u32[]{:S(2)}) copy-start(f32[1,8,1024]{2,1,0:T(8,128)} %param.10) | copy-start | bytes 98308
  108.2 11.8 %copy-start.3 = (f32[1,8,1024]{2,1,0:T(8,128)S(1)}, f32[1,8,1024]{2,1,0:T(8,128)}, u32[]{:S(2)}) copy-start(f32[1,8,1024]{2,1,0:T(8,128)} %param.11) | copy-start | bytes 98308
  109.5 28.0 %all-to-all-start.2 = ((bf16[16,32,512]{2,1,0:T(8,128)(2,1)}), bf16[16,32,512]{2,1,0:T(8,128)(2,1)S(1)}, u32[]{:S(2)}, u32[]{:S(2)}) async-start(bf16[16,32,512]{2,1,0:T(8,128)(2,1)} %bitcast.6), calls=%async_computation.2 | async-start | bytes 1048576 | tf_op jit(solution)/shard_map/all_to_all | solution.py:21
  138.2 7.7 %all-to-all-start.3 = ((f32[4,8,512]{2,1,0:T(8,128)}), f32[4,8,512]{2,1,0:T(8,128)S(1)}, u32[]{:S(2)}, u32[]{:S(2)}) async-start(f32[4,8,512]{2,1,0:T(8,128)} %bitcast.7), calls=%async_computation.3 | async-start | bytes 131072 | tf_op jit(solution)/shard_map/all_to_all | solution.py:21
  141.8 23.3 %collective-permute-start.4 = (bf16[256,1792]{1,0:T(8,128)(2,1)S(1)}, bf16[256,1792]{1,0:T(8,128)(2,1)}, u32[]{:S(2)}, u32[]{:S(2)}) collective-permute-start(bf16[256,1792]{1,0:T(8,128)(2,1)S(1)} %collective-permute-done.2), channel_id=1, source_target_pairs={{0,8},{8,0},{16,24},{24,16},{1,9},{9,1},{17,25},{25,17},{2,10},{10... | collective-permute-start | bytes 2752520 | tf_op jit(solution)/shard_map/ppermute | solution.py:37
  149.4 13.2 %all-to-all-start.4 = ((bf16[8,8,1024]{2,1,0:T(8,128)(2,1)}), bf16[8,8,1024]{2,1,0:T(8,128)(2,1)S(1)}, u32[]{:S(2)}, u32[]{:S(2)}) async-start(bf16[8,8,1024]{2,1,0:T(8,128)(2,1)} %broadcast_in_dim.4), calls=%async_computation.4 | async-start | bytes 262144 | tf_op jit(solution)/shard_map/all_to_all | solution.py:21
  163.6 1.5 copy-start.1

commit v4 on v3

--- a/solution.py
+++ b/solution.py
@@ -84,8 +84,8 @@
         ]
         return jnp.concatenate(parts).reshape(groups, -1, ranks)
 
-    near = summed(exchange(project(own), fsdp))
-    near, act_pair = lax.optimization_barrier((near, act_pair))
+    near, act_pair = lax.optimization_barrier((project(own), act_pair))
+    near = summed(exchange(near, fsdp))
     far = summed(exchange(project(after(other, near)), fsdp))
     pair_own = shift(own, partner)
     pair_other = shift(other, partner)

time: 194 us -> 193 us (level)
  blocking collectives: 75.9 us -> 99.9 us
  starting transfers between devices: 53.8 us -> 40.8 us
  waiting for transfers between devices: 41.4 us -> 31.3 us
    all_to_all x0 -> x1, blocking collectives: none -> 23.5 us  [exchange(): return lax.all_to_all(block, axes, 0, 0, tiled=True)]
    all_to_all x5 -> x4, starting transfers between devices: 38.4 us -> 25.4 us  [exchange(): return lax.all_to_all(block, axes, 0, 0, tiled=True)]
    all_to_all x5 -> x4, waiting for transfers between devices: 40.5 us -> 31.3 us  [exchange(): return lax.all_to_all(block, axes, 0, 0, tiled=True)]
  transfers between devices with their start and end apart: 10 -> 9, of which waited for: 6 -> 4; matrix products, arithmetic and copies ran while one was open for 6% -> 6% of each run, Pallas kernels for 0% -> 0%
where the time goes in v4:
time: 193 us; the launch traced here: 192 us
  blocking collectives  99.9 us (52%)
  starting transfers between devices  40.8 us (21%)
  waiting for transfers between devices  31.3 us (16%)
  matrix products  9.05 us (5%)
  local copies, waits for them, and re-layouts  7.91 us (4%)
  other arithmetic  2.24 us (1%)
    all_gather x4, blocking collectives, gather(): return lax.all_gather(block, axes, axis=0, tiled=True)  68.5 us
    all_to_all x4, waiting for transfers between devices, exchange(): return lax.all_to_all(block, axes, 0, 0, tiled=True)  31.3 us
    all_to_all x4, starting transfers between devices, exchange(): return lax.all_to_all(block, axes, 0, 0, tiled=True)  25.4 us
    all_to_all x1, blocking collectives, exchange(): return lax.all_to_all(block, axes, 0, 0, tiled=True)  23.5 us
    ppermute x5, starting transfers between devices, shift(): return lax.ppermute(block, 'x', [(i, j) for i, j in enumerate(pairs)])  15.4 us
    dot_general x10, matrix products, contract(): lax.dot_general(left, right, (dims, ((), ())), preferred_element_type=jnp...  9.05 us
    all_gather x2, blocking collectives, shards(): lax.all_gather(column[:, part * 4:part * 4 + 4], 'core', axis=1)  7.98 us
  transfers between devices with their start and end apart: 9, of which 4 were waited for; matrix products, arithmetic and copies ran while one was open for 6% of the time, Pallas kernels for 0%

profile of v4, /device:TPU:1, one launch (start us, length us, event | category | flops | bytes accessed | tf_op | source)
XLA Modules:
  0.0 192.3 jit_solution(4428686035401182795)
XLA Ops:
  0.6 4.0 %collective-permute-start = (bf16[384,1792]{1,0:T(8,128)(2,1)}, bf16[384,1792]{1,0:T(8,128)(2,1)S(1)}, u32[]{:S(2)}, u32[]{:S(2)}) collective-permute-start(bf16[384,1792]{1,0:T(8,128)(2,1)} %param.7), channel_id=1, source_target_pairs={{0,8},{8,0},{16,24},{24,16},{1,9},{9,1},{17,25},{25,17},{2,10},{10... | collective-permute-start | bytes 4128776 | tf_op jit(solution)/shard_map/ppermute | solution.py:37
  4.6 1.9 collective-permute-start.1
  6.5 11.5 %all_gather.24 = bf16[32,1792]{1,0:T(8,128)(2,1)S(1)} all-gather(bf16[16,1792]{1,0:T(8,128)(2,1)} %param.8), channel_id=1, replica_groups=mesh['zh'=2,'y'=8,'x'=4,'zl'=4,'core'=2] {'zh'}, dimensions={0}, use_global_device_ids=true | all-gather | bytes 172032 | tf_op jit(solution)/shard_map/all_gather | solution.py:63
  18.0 23.3 %all_gather.25 = bf16[256,1792]{1,0:T(8,128)(2,1)S(1)} all-gather(bf16[32,1792]{1,0:T(8,128)(2,1)S(1)} %all_gather.24), channel_id=1, replica_groups=mesh['zh'=2,'y'=8,'x'=4,'zl'=4,'core'=2] {'y'}, dimensions={0}, use_global_device_ids=true | all-gather | bytes 1032192 | tf_op jit(solution)/shard_map/all_gather | solution.py:63
  41.4 4.3 %collective-permute-start.2 = (bf16[256,1792]{1,0:T(8,128)(2,1)S(1)}, bf16[256,1792]{1,0:T(8,128)(2,1)S(1)}, u32[]{:S(2)}, u32[]{:S(2)}) collective-permute-start(bf16[256,1792]{1,0:T(8,128)(2,1)S(1)} %all_gather.25), channel_id=1, source_target_pairs={{0,24},{8,16},{16,8},{24,0},{1,25},{9,17},{17,9},{25,1},{2,26},{10... | collective-permute-start | bytes 2752520 | tf_op jit(solution)/shard_map/ppermute | solution.py:37
  45.6 1.9 convolution_convert_fusion.3
  47.6 0.6 convolution_convert_fusion.2
  48.2 23.5 %all_to_all.25 = bf16[8,96,256]{2,1,0:T(8,128)(2,1)S(1)} all-to-all(bf16[8,96,256]{2,1,0:T(8,128)(2,1)S(1)} %bitcast.62), channel_id=1, replica_groups=mesh['zh'=2,'y'=8,'x'=4,'zl'=4,'core'=2] {'zl','core'}, dimensions={0} | all-to-all | bytes 786432 | tf_op jit(solution)/shard_map/all_to_all | solution.py:21
  71.7 0.7 fusion.5
  72.4 0.7 fusion.6
  73.1 0.9 copy.22
  74.0 4.3 %all-to-all-start.1 = ((bf16[8,96,256]{2,1,0:T(8,128)(2,1)}), bf16[8,96,256]{2,1,0:T(8,128)(2,1)S(1)}, u32[]{:S(2)}, u32[]{:S(2)}) async-start(bf16[8,96,256]{2,1,0:T(8,128)(2,1)} %bitcast.4), calls=%async_computation.1 | async-start | bytes 786432 | tf_op jit(solution)/shard_map/all_to_all | solution.py:21
  78.3 1.9 collective-permute-start.3
  80.3 9.8 %all-to-all-done.1 = bf16[8,96,256]{2,1,0:T(8,128)(2,1)S(1)} async-done(((bf16[8,96,256]{2,1,0:T(8,128)(2,1)}), bf16[8,96,256]{2,1,0:T(8,128)(2,1)S(1)}, u32[]{:S(2)}, u32[]{:S(2)}) %all-to-all-start.1) | async-done | bytes 393248 | tf_op jit(solution)/shard_map/all_to_all | solution.py:21
  90.1 16.4 %all_gather.26 = bf16[768,512]{1,0:T(8,128)(2,1)S(1)} all-gather(bf16[96,512]{1,0:T(8,128)(2,1)S(1)} %pad_maximum_fusion.4), channel_id=1, replica_groups=mesh['zh'=2,'y'=8,'x'=4,'zl'=4,'core'=2] {'zl','core'}, dimensions={0}, use_global_device_ids=true | all-gather | bytes 884736 | tf_op jit(solution)/shard_map/all_gather | solution.py:63
  106.6 0.5 convolution_bitcast_fusion
  107.1 1.3 fusion.4
  108.3 10.4 %all-to-all-start.2 = ((bf16[16,32,512]{2,1,0:T(8,128)(2,1)}), bf16[16,32,512]{2,1,0:T(8,128)(2,1)S(1)}, u32[]{:S(2)}, u32[]{:S(2)}) async-start(bf16[16,32,512]{2,1,0:T(8,128)(2,1)} %bitcast.6), calls=%async_computation.2 | async-start | bytes 1048576 | tf_op jit(solution)/shard_map/all_to_all | solution.py:21
  118.8 0.2 reshape_squeeze.6
  119.0 0.2 reshape_squeeze.7
  119.3 17.1 %all-to-all-done.2 = bf16[16,32,512]{2,1,0:T(8,128)(2,1)S(1)} async-done(((bf16[16,32,512]{2,1,0:T(8,128)(2,1)}), bf16[16,32,512]{2,1,0:T(8,128)(2,1)S(1)}, u32[]{:S(2)}, u32[]{:S(2)}) %all-to-all-start.2) | async-done | bytes 524320 | tf_op jit(solution)/shard_map/all_to_all | solution.py:21
  136.4 0.7 convert_reduce_fusion
  137.1 3.3 %all-to-all-start.3 = ((f32[4,8,512]{2,1,0:T(8,128)}), f32[4,8,512]{2,1,0:T(8,128)S(1)}, u32[]{:S(2)}, u32[]{:S(2)}) async-start(f32[4,8,512]{2,1,0:T(8,128)} %bitcast.7), calls=%async_computation.3 | async-start | bytes 131072 | tf_op jit(solution)/shard_map/all_to_all | solution.py:21
  140.7 3.3 %collective-permute-start.4 = (bf16[256,1792]{1,0:T(8,128)(2,1)S(1)}, bf16[256,1792]{1,0:T(8,128)(2,1)}, u32[]{:S(2)}, u32[]{:S(2)}) collective-permute-start(bf16[256,1792]{1,0:T(8,128)(2,1)S(1)} %collective-permute-done.2), channel_id=1, source_target_pairs={{0,8},{8,0},{16,24},{24,16},{1,9},{9,1},{17,25},{25,17},{2,10},{10... | collective-permute-start | bytes 2752520 | tf_op jit(solution)/shard_map/ppermute | solution.py:37
  144.1 0.8 all-to-all-done.3
  144.9 0.2 add.85
  145.2 0.2 add.86
  145.5 0.7 fusion.9
  146.2 0.2 fusion.26
  146.5 0.2 copy.21
  146.7 0.3 mul.123
  147.3 0.3 mul.130
  147.7 0.7 broadcast_in_dim.4
  148.3 7.4 %all-to-all-start.4 = ((bf16[8,8,1024]{2,1,0:T(8,128)(2,1)}), bf16[8,8,1024]{2,1,0:T(8,128)(2,1)S(1)}, u32[]{:S(2)}, u32[]{:S(2)}) async-start(bf16[8,8,1024]{2,1,0:T(8,128)(2,1)} %broadcast_in_dim.4), calls=%async_computation.4 | async-start | bytes 262144 | tf_op jit(solution)/shard_map/all_to_all | solution.py:21
  155.7 0.2 maximum_bitcast_fusion.1
  155.9 0.9 broadcast_in_dim_reshape.7
  156.8 0.2 maximum_bitcast_fusion
  157.0 0.9 broadcast_in_dim_reshape.6
  157.9 3.7 %all-to-all-done.4 = bf16[8,8,1024]{2,1,0:T(8,128)(2,1)S(1)} async-done(((bf16[8,8,1024]{2,1,0:T(8,128)(2,1)}), bf16[8,8,1024]{2,1,0:T(8,128)(2,1)S(1)}, u32[]{:S(2)}, u32[]{:S(2)}) %all-to-all-start.4) | async-done | bytes 131104 | tf_op jit(solution)/shard_map/all_to_all | solution.py:21
  161.6 0.3 constant_dynamic-slice_fusion
  161.9 0.3 fusion.21
  162.2 0.3 convolution_add_fusion.2
  162.5 1.5 convolution_add_fusion.1
  164.0 1.5 fusion.3
  165.5 17.2 %all-gather = bf16[32,8,1792]{2,1,0:T(8,128)(2,1)S(1)} all-gather(bf16[8,8,1792]{2,1,0:T(8,128)(2,1)S(1)} %fusion.3), channel_id=2, replica_groups=mesh['zh'=2,'y'=8,'x'=4,'zl'=4,'core'=2] {'zl'}, dimensions={0}, use_global_device_ids=true | all-gather | bytes 1146880 | tf_op jit(solution)/shard_map/all_gather | solution.py:63
  182.8 5.5 %all-gather.1 = bf16[4,8,8,1792]{3,2,1,0:T(8,128)(2,1)S(1)} all-gather(bf16[4,4,8,1792]{3,2,1,0:T(8,128)(2,1)S(1)} %get-tuple-element.11), channel_id=3, replica_groups=mesh['zh'=2,'y'=8,'x'=4,'zl'=4,'core'=2] {'core'}, dimensions={1}, use_global_device_ids=true | all-gather | bytes 1376256 | tf_op jit(solution)/shard_map/all_gather | solution.py:128
  188.3 2.5 %all-gather.2 = bf16[4,8,8,1792]{3,2,1,0:T(8,128)(2,1)S(1)} all-gather(bf16[4,4,8,1792]{3,2,1,0:T(8,128)(2,1)S(1)} %get-tuple-element.12), channel_id=4, replica_groups=mesh['zh'=2,'y'=8,'x'=4,'zl'=4,'core'=2] {'core'}, dimensions={1}, use_global_device_ids=true | all-gather | bytes 1376256 | tf_op jit(solution)/shard_map/all_gather | solution.py:128
  190.9 1.4 copy.24
  (35 shorter events, 1.4 us)
Async XLA Ops:
  0.6 46.9 %collective-permute-start = (bf16[384,1792]{1,0:T(8,128)(2,1)}, bf16[384,1792]{1,0:T(8,128)(2,1)S(1)}, u32[]{:S(2)}, u32[]{:S(2)}) collective-permute-start(bf16[384,1792]{1,0:T(8,128)(2,1)} %param.7), channel_id=1, source_target_pairs={{0,8},{8,0},{16,24},{24,16},{1,9},{9,1},{17,25},{25,17},{2,10},{10... | collective-permute-start | bytes 4128776 | tf_op jit(solution)/shard_map/ppermute | solution.py:37
  4.6 43.6 %collective-permute-start.1 = (bf16[384,512]{1,0:T(8,128)(2,1)}, bf16[384,512]{1,0:T(8,128)(2,1)S(1)}, u32[]{:S(2)}, u32[]{:S(2)}) collective-permute-start(bf16[384,512]{1,0:T(8,128)(2,1)} %param.6), channel_id=1, source_target_pairs={{0,8},{8,0},{16,24},{24,16},{1,9},{9,1},{17,25},{25,17},{2,10},{10... | collective-permute-start | bytes 1179656 | tf_op jit(solution)/shard_map/ppermute | solution.py:37
  41.4 30.3 %collective-permute-start.2 = (bf16[256,1792]{1,0:T(8,128)(2,1)S(1)}, bf16[256,1792]{1,0:T(8,128)(2,1)S(1)}, u32[]{:S(2)}, u32[]{:S(2)}) collective-permute-start(bf16[256,1792]{1,0:T(8,128)(2,1)S(1)} %all_gather.25), channel_id=1, source_target_pairs={{0,24},{8,16},{16,8},{24,0},{1,25},{9,17},{17,9},{25,1},{2,26},{10... | collective-permute-start | bytes 2752520 | tf_op jit(solution)/shard_map/ppermute | solution.py:37
  48.1 23.6 %copy-start.4 = (bf16[384,1792]{1,0:T(8,128)(2,1)S(1)}, bf16[384,1792]{1,0:T(8,128)(2,1)}, u32[]{:S(2)}) copy-start(bf16[384,1792]{1,0:T(8,128)(2,1)} %param.7) | copy-start | bytes 4128772
  74.0 32.6 %copy-start = (bf16[384,512]{1,0:T(8,128)(2,1)S(1)}, bf16[384,512]{1,0:T(8,128)(2,1)}, u32[]{:S(2)}) copy-start(bf16[384,512]{1,0:T(8,128)(2,1)} %param.6) | copy-start | bytes 1179652
  74.0 16.0 %all-to-all-start.1 = ((bf16[8,96,256]{2,1,0:T(8,128)(2,1)}), bf16[8,96,256]{2,1,0:T(8,128)(2,1)S(1)}, u32[]{:S(2)}, u32[]{:S(2)}) async-start(bf16[8,96,256]{2,1,0:T(8,128)(2,1)} %bitcast.4), calls=%async_computation.1 | async-start | bytes 786432 | tf_op jit(solution)/shard_map/all_to_all | solution.py:21
  78.3 28.2 %collective-permute-start.3 = (bf16[256,1792]{1,0:T(8,128)(2,1)S(1)}, bf16[256,1792]{1,0:T(8,128)(2,1)}, u32[]{:S(2)}, u32[]{:S(2)}) collective-permute-start(bf16[256,1792]{1,0:T(8,128)(2,1)S(1)} %all_gather.25), channel_id=1, source_target_pairs={{0,8},{8,0},{16,24},{24,16},{1,9},{9,1},{17,25},{25,17},{2,10},{10... | collective-permute-start | bytes 2752520 | tf_op jit(solution)/shard_map/ppermute | solution.py:37
  107.1 11.7 %copy-start.2 = (f32[1,8,1024]{2,1,0:T(8,128)S(1)}, f32[1,8,1024]{2,1,0:T(8,128)}, u32[]{:S(2)}) copy-start(f32[1,8,1024]{2,1,0:T(8,128)} %param.10) | copy-start | bytes 98308
  107.1 11.9 %copy-start.3 = (f32[1,8,1024]{2,1,0:T(8,128)S(1)}, f32[1,8,1024]{2,1,0:T(8,128)}, u32[]{:S(2)}) copy-start(f32[1,8,1024]{2,1,0:T(8,128)} %param.11) | copy-start | bytes 98308
  108.3 28.1 %all-to-all-start.2 = ((bf16[16,32,512]{2,1,0:T(8,128)(2,1)}), bf16[16,32,512]{2,1,0:T(8,128)(2,1)S(1)}, u32[]{:S(2)}, u32[]{:S(2)}) async-start(bf16[16,32,512]{2,1,0:T(8,128)(2,1)} %bitcast.6), calls=%async_computation.2 | async-start | bytes 1048576 | tf_op jit(solution)/shard_map/all_to_all | solution.py:21
  137.1 7.7 %all-to-all-start.3 = ((f32[4,8,512]{2,1,0:T(8,128)}), f32[4,8,512]{2,1,0:T(8,128)S(1)}, u32[]{:S(2)}, u32[]{:S(2)}) async-start(f32[4,8,512]{2,1,0:T(8,128)} %bitcast.7), calls=%async_computation.3 | async-start | bytes 131072 | tf_op jit(solution)/shard_map/all_to_all | solution.py:21
  140.7 23.3 %collective-permute-start.4 = (bf16[256,1792]{1,0:T(8,128)(2,1)S(1)}, bf16[256,1792]{1,0:T(8,128)(2,1)}, u32[]{:S(2)}, u32[]{:S(2)}) collective-permute-start(bf16[256,1792]{1,0:T(8,128)(2,1)S(1)} %collective-permute-done.2), channel_id=1, source_target_pairs={{0,8},{8,0},{16,24},{24,16},{1,9},{9,1},{17,25},{25,17},{2,10},{10... | collective-permute-start | bytes 2752520 | tf_op jit(solution)/shard_map/ppermute | solution.py:37
  148.3 13.2 %all-to-all-start.4 = ((bf16[8,8,1024]{2,1,0:T(8,128)(2,1)}), bf16[8,8,1024]{2,1,0:T(8,128)(2,1)S(1)}, u32[]{:S(2)}, u32[]{:S(2)}) async-start(bf16[8,8,1024]{2,1,0:T(8,128)(2,1)} %broadcast_in_dim.4), calls=%async_computation.4 | async-start | bytes 262144 | tf_op jit(solution)/shard_map/all_to_all | solution.py:21
  162.5 1.5 copy-start.1

commit v5 on v3

--- a/solution.py
+++ b/solution.py
@@ -85,7 +85,6 @@
         return jnp.concatenate(parts).reshape(groups, -1, ranks)
 
     near = summed(exchange(project(own), fsdp))
-    near, act_pair = lax.optimization_barrier((near, act_pair))
     far = summed(exchange(project(after(other, near)), fsdp))
     pair_own = shift(own, partner)
     pair_other = shift(other, partner)
@@ -93,11 +92,11 @@
     owned = jnp.concatenate(
         (jnp.where(low_place, near, far), jnp.where(low_place, far, near)), axis=1
     ).astype(jnp.bfloat16)
-    projected = after(gather(owned, fsdp), pair_own)
+    projected = gather(owned, fsdp)
 
     low = contract(activations, projected[:tokens], ((0,), (0,)))
     low += contract(act_pair, projected[tokens:], ((0,), (0,)))
-    low = low.astype(jnp.bfloat16)
+    low = after(low.astype(jnp.bfloat16), pair_own)
     low = summed(exchange(low.reshape(16, -1, 2 * ranks), rest))
     low = exchange(low.reshape(4, rows, 2 * ranks), "x")
     low_grad = jnp.concatenate((low[0] + low[3], low[1] + low[2]), axis=1)

time: 194 us -> 194 us (level)
  blocking collectives: 75.9 us -> 98.9 us
  starting transfers between devices: 53.8 us -> 43 us
  waiting for transfers between devices: 41.4 us -> 30.7 us
  matrix products: 10.4 us -> 8.22 us
    all_to_all x0 -> x1, blocking collectives: none -> 23.5 us  [exchange(): return lax.all_to_all(block, axes, 0, 0, tiled=True)]
    all_to_all x5 -> x4, waiting for transfers between devices: 40.5 us -> 27.3 us  [exchange(): return lax.all_to_all(block, axes, 0, 0, tiled=True)]
    all_to_all x5 -> x4, starting transfers between devices: 38.4 us -> 26.8 us  [exchange(): return lax.all_to_all(block, axes, 0, 0, tiled=True)]
    ppermute x5, waiting for transfers between devices: 0.87 us -> 3.46 us  [shift(): return lax.ppermute(block, 'x', [(i, j) for i, j in enumerate(pairs)])]
    dot_general x10, matrix products: 10.4 us -> 8.22 us  [contract(): lax.dot_general(left, right, (dims, ((), ())), preferred_element_type=jnp...]
  transfers between devices with their start and end apart: 10 -> 9, of which waited for: 6 -> 5; matrix products, arithmetic and copies ran while one was open for 6% -> 6% of each run, Pallas kernels for 0% -> 0%
where the time goes in v5:
time: 194 us; the launch traced here: 193 us
  blocking collectives  98.9 us (51%)
  starting transfers between devices  43 us (22%)
  waiting for transfers between devices  30.7 us (16%)
  local copies, waits for them, and re-layouts  8.92 us (5%)
  matrix products  8.22 us (4%)
  other arithmetic  2.24 us (1%)
    all_gather x4, blocking collectives, gather(): return lax.all_gather(block, axes, axis=0, tiled=True)  68.5 us
    all_to_all x4, waiting for transfers between devices, exchange(): return lax.all_to_all(block, axes, 0, 0, tiled=True)  27.3 us
    all_to_all x4, starting transfers between devices, exchange(): return lax.all_to_all(block, axes, 0, 0, tiled=True)  26.8 us
    all_to_all x1, blocking collectives, exchange(): return lax.all_to_all(block, axes, 0, 0, tiled=True)  23.5 us
    ppermute x5, starting transfers between devices, shift(): return lax.ppermute(block, 'x', [(i, j) for i, j in enumerate(pairs)])  16.3 us
    dot_general x10, matrix products, contract(): lax.dot_general(left, right, (dims, ((), ())), preferred_element_type=jnp...  8.22 us
    all_gather x2, blocking collectives, shards(): lax.all_gather(column[:, part * 4:part * 4 + 4], 'core', axis=1)  6.97 us
  transfers between devices with their start and end apart: 9, of which 5 were waited for; matrix products, arithmetic and copies ran while one was open for 6% of the time, Pallas kernels for 0%

profile of v5, /device:TPU:1, one launch (start us, length us, event | category | flops | bytes accessed | tf_op | source)
XLA Modules:
  0.0 193.2 jit_solution(7907000671504976661)
XLA Ops:
  0.6 4.0 %collective-permute-start = (bf16[384,1792]{1,0:T(8,128)(2,1)}, bf16[384,1792]{1,0:T(8,128)(2,1)S(1)}, u32[]{:S(2)}, u32[]{:S(2)}) collective-permute-start(bf16[384,1792]{1,0:T(8,128)(2,1)} %param.7), channel_id=1, source_target_pairs={{0,8},{8,0},{16,24},{24,16},{1,9},{9,1},{17,25},{25,17},{2,10},{10... | collective-permute-start | bytes 4128776 | tf_op jit(solution)/shard_map/ppermute | solution.py:37
  4.6 11.3 %all_gather.24 = bf16[32,1792]{1,0:T(8,128)(2,1)S(1)} all-gather(bf16[16,1792]{1,0:T(8,128)(2,1)} %param.8), channel_id=1, replica_groups=mesh['zh'=2,'y'=8,'x'=4,'zl'=4,'core'=2] {'zh'}, dimensions={0}, use_global_device_ids=true | all-gather | bytes 172032 | tf_op jit(solution)/shard_map/all_gather | solution.py:63
  15.9 23.0 %all_gather.25 = bf16[256,1792]{1,0:T(8,128)(2,1)S(1)} all-gather(bf16[32,1792]{1,0:T(8,128)(2,1)S(1)} %all_gather.24), channel_id=1, replica_groups=mesh['zh'=2,'y'=8,'x'=4,'zl'=4,'core'=2] {'y'}, dimensions={0}, use_global_device_ids=true | all-gather | bytes 1032192 | tf_op jit(solution)/shard_map/all_gather | solution.py:63
  38.9 3.7 %collective-permute-start.1 = (bf16[256,1792]{1,0:T(8,128)(2,1)S(1)}, bf16[256,1792]{1,0:T(8,128)(2,1)S(1)}, u32[]{:S(2)}, u32[]{:S(2)}) collective-permute-start(bf16[256,1792]{1,0:T(8,128)(2,1)S(1)} %all_gather.25), channel_id=1, source_target_pairs={{0,24},{8,16},{16,8},{24,0},{1,25},{9,17},{17,9},{25,1},{2,26},{10... | collective-permute-start | bytes 2752520 | tf_op jit(solution)/shard_map/ppermute | solution.py:37
  42.6 1.9 convolution_convert_fusion.3
  44.5 0.6 convolution_convert_fusion.2
  45.1 23.5 %all_to_all.25 = bf16[8,96,256]{2,1,0:T(8,128)(2,1)S(1)} all-to-all(bf16[8,96,256]{2,1,0:T(8,128)(2,1)S(1)} %bitcast.62), channel_id=1, replica_groups=mesh['zh'=2,'y'=8,'x'=4,'zl'=4,'core'=2] {'zl','core'}, dimensions={0} | all-to-all | bytes 786432 | tf_op jit(solution)/shard_map/all_to_all | solution.py:21
  68.7 0.7 fusion.6
  69.3 0.7 fusion.7
  70.1 0.9 copy.24
  71.0 4.2 %all-to-all-start.1 = ((bf16[8,96,256]{2,1,0:T(8,128)(2,1)}), bf16[8,96,256]{2,1,0:T(8,128)(2,1)S(1)}, u32[]{:S(2)}, u32[]{:S(2)}) async-start(bf16[8,96,256]{2,1,0:T(8,128)(2,1)} %bitcast.4), calls=%async_computation.1 | async-start | bytes 786432 | tf_op jit(solution)/shard_map/all_to_all | solution.py:21
  75.2 2.2 %collective-permute-start.3 = (bf16[256,1792]{1,0:T(8,128)(2,1)S(1)}, bf16[256,1792]{1,0:T(8,128)(2,1)}, u32[]{:S(2)}, u32[]{:S(2)}) collective-permute-start(bf16[256,1792]{1,0:T(8,128)(2,1)S(1)} %all_gather.25), channel_id=1, source_target_pairs={{0,8},{8,0},{16,24},{24,16},{1,9},{9,1},{17,25},{25,17},{2,10},{10... | collective-permute-start | bytes 2752520 | tf_op jit(solution)/shard_map/ppermute | solution.py:37
  77.4 3.1 %collective-permute-start.2 = (bf16[384,512]{1,0:T(8,128)(2,1)S(1)}, bf16[384,512]{1,0:T(8,128)(2,1)S(1)}, u32[]{:S(2)}, u32[]{:S(2)}) collective-permute-start(bf16[384,512]{1,0:T(8,128)(2,1)S(1)} %copy-done), channel_id=1, source_target_pairs={{0,8},{8,0},{16,24},{24,16},{1,9},{9,1},{17,25},{25,17},{2,10},{10... | collective-permute-start | bytes 1179656 | tf_op jit(solution)/shard_map/ppermute | solution.py:37
  80.5 6.4 %all-to-all-done.1 = bf16[8,96,256]{2,1,0:T(8,128)(2,1)S(1)} async-done(((bf16[8,96,256]{2,1,0:T(8,128)(2,1)}), bf16[8,96,256]{2,1,0:T(8,128)(2,1)S(1)}, u32[]{:S(2)}, u32[]{:S(2)}) %all-to-all-start.1) | async-done | bytes 393248 | tf_op jit(solution)/shard_map/all_to_all | solution.py:21
  87.0 16.4 %all_gather.26 = bf16[768,512]{1,0:T(8,128)(2,1)S(1)} all-gather(bf16[96,512]{1,0:T(8,128)(2,1)S(1)} %pad_maximum_fusion.4), channel_id=1, replica_groups=mesh['zh'=2,'y'=8,'x'=4,'zl'=4,'core'=2] {'zl','core'}, dimensions={0}, use_global_device_ids=true | all-gather | bytes 884736 | tf_op jit(solution)/shard_map/all_gather | solution.py:63
  103.4 0.5 fusion.9
  103.9 3.4 %collective-permute-done.2 = bf16[384,512]{1,0:T(8,128)(2,1)S(1)} collective-permute-done((bf16[384,512]{1,0:T(8,128)(2,1)S(1)}, bf16[384,512]{1,0:T(8,128)(2,1)S(1)}, u32[]{:S(2)}, u32[]{:S(2)}) %collective-permute-start.2) | collective-permute-done | bytes 393248 | tf_op jit(solution)/shard_map/ppermute | solution.py:37
  107.3 0.5 fusion.5
  107.8 1.0 copy.25
  108.8 10.3 %all-to-all-start.2 = ((bf16[16,32,512]{2,1,0:T(8,128)(2,1)}), bf16[16,32,512]{2,1,0:T(8,128)(2,1)S(1)}, u32[]{:S(2)}, u32[]{:S(2)}) async-start(bf16[16,32,512]{2,1,0:T(8,128)(2,1)} %bitcast.6), calls=%async_computation.2 | async-start | bytes 1048576 | tf_op jit(solution)/shard_map/all_to_all | solution.py:21
  119.2 0.2 reshape_squeeze.6
  119.4 0.2 reshape_squeeze.7
  119.8 16.4 %all-to-all-done.2 = bf16[16,32,512]{2,1,0:T(8,128)(2,1)S(1)} async-done(((bf16[16,32,512]{2,1,0:T(8,128)(2,1)}), bf16[16,32,512]{2,1,0:T(8,128)(2,1)S(1)}, u32[]{:S(2)}, u32[]{:S(2)}) %all-to-all-start.2) | async-done | bytes 524320 | tf_op jit(solution)/shard_map/all_to_all | solution.py:21
  136.2 0.7 convert_reduce_fusion
  136.9 3.3 %all-to-all-start.3 = ((f32[4,8,512]{2,1,0:T(8,128)}), f32[4,8,512]{2,1,0:T(8,128)S(1)}, u32[]{:S(2)}, u32[]{:S(2)}) async-start(f32[4,8,512]{2,1,0:T(8,128)} %bitcast.7), calls=%async_computation.3 | async-start | bytes 131072 | tf_op jit(solution)/shard_map/all_to_all | solution.py:21
  140.5 3.3 %collective-permute-start.4 = (bf16[256,1792]{1,0:T(8,128)(2,1)S(1)}, bf16[256,1792]{1,0:T(8,128)(2,1)}, u32[]{:S(2)}, u32[]{:S(2)}) collective-permute-start(bf16[256,1792]{1,0:T(8,128)(2,1)S(1)} %collective-permute-done.1), channel_id=1, source_target_pairs={{0,8},{8,0},{16,24},{24,16},{1,9},{9,1},{17,25},{25,17},{2,10},{10... | collective-permute-start | bytes 2752520 | tf_op jit(solution)/shard_map/ppermute | solution.py:37
  143.8 0.8 all-to-all-done.3
  144.7 0.2 add.86
  144.9 0.2 add.87
  145.2 0.7 fusion.11
  146.5 0.3 mul.123
  147.1 0.3 mul.130
  147.4 0.7 broadcast_in_dim.4
  148.1 8.9 %all-to-all-start.4 = ((bf16[8,8,1024]{2,1,0:T(8,128)(2,1)}), bf16[8,8,1024]{2,1,0:T(8,128)(2,1)S(1)}, u32[]{:S(2)}, u32[]{:S(2)}) async-start(bf16[8,8,1024]{2,1,0:T(8,128)(2,1)} %broadcast_in_dim.4), calls=%async_computation.4 | async-start | bytes 262144 | tf_op jit(solution)/shard_map/all_to_all | solution.py:21
  157.1 0.2 maximum_bitcast_fusion.1
  157.3 0.9 broadcast_in_dim_reshape.7
  158.1 0.2 maximum_bitcast_fusion
  158.4 0.9 broadcast_in_dim_reshape.6
  159.2 3.6 %all-to-all-done.4 = bf16[8,8,1024]{2,1,0:T(8,128)(2,1)S(1)} async-done(((bf16[8,8,1024]{2,1,0:T(8,128)(2,1)}), bf16[8,8,1024]{2,1,0:T(8,128)(2,1)S(1)}, u32[]{:S(2)}, u32[]{:S(2)}) %all-to-all-start.4) | async-done | bytes 131104 | tf_op jit(solution)/shard_map/all_to_all | solution.py:21
  162.9 0.3 constant_dynamic-slice_fusion
  163.2 0.3 fusion.23
  163.5 0.3 convolution_add_fusion.2
  163.8 1.5 convolution_add_fusion.1
  165.3 1.5 fusion.3
  166.8 17.8 %all-gather = bf16[32,8,1792]{2,1,0:T(8,128)(2,1)S(1)} all-gather(bf16[8,8,1792]{2,1,0:T(8,128)(2,1)S(1)} %fusion.3), channel_id=2, replica_groups=mesh['zh'=2,'y'=8,'x'=4,'zl'=4,'core'=2] {'zl'}, dimensions={0}, use_global_device_ids=true | all-gather | bytes 1146880 | tf_op jit(solution)/shard_map/all_gather | solution.py:63
  184.7 4.5 %all-gather.1 = bf16[4,8,8,1792]{3,2,1,0:T(8,128)(2,1)S(1)} all-gather(bf16[4,4,8,1792]{3,2,1,0:T(8,128)(2,1)S(1)} %get-tuple-element.7), channel_id=3, replica_groups=mesh['zh'=2,'y'=8,'x'=4,'zl'=4,'core'=2] {'core'}, dimensions={1}, use_global_device_ids=true | all-gather | bytes 1376256 | tf_op jit(solution)/shard_map/all_gather | solution.py:127
  189.2 2.5 %all-gather.2 = bf16[4,8,8,1792]{3,2,1,0:T(8,128)(2,1)S(1)} all-gather(bf16[4,4,8,1792]{3,2,1,0:T(8,128)(2,1)S(1)} %get-tuple-element.8), channel_id=4, replica_groups=mesh['zh'=2,'y'=8,'x'=4,'zl'=4,'core'=2] {'core'}, dimensions={1}, use_global_device_ids=true | all-gather | bytes 1376256 | tf_op jit(solution)/shard_map/all_gather | solution.py:127
  191.8 1.4 copy.27
  (36 shorter events, 1.8 us)
Async XLA Ops:
  0.6 43.9 %collective-permute-start = (bf16[384,1792]{1,0:T(8,128)(2,1)}, bf16[384,1792]{1,0:T(8,128)(2,1)S(1)}, u32[]{:S(2)}, u32[]{:S(2)}) collective-permute-start(bf16[384,1792]{1,0:T(8,128)(2,1)} %param.7), channel_id=1, source_target_pairs={{0,8},{8,0},{16,24},{24,16},{1,9},{9,1},{17,25},{25,17},{2,10},{10... | collective-permute-start | bytes 4128776 | tf_op jit(solution)/shard_map/ppermute | solution.py:37
  38.9 29.8 %collective-permute-start.1 = (bf16[256,1792]{1,0:T(8,128)(2,1)S(1)}, bf16[256,1792]{1,0:T(8,128)(2,1)S(1)}, u32[]{:S(2)}, u32[]{:S(2)}) collective-permute-start(bf16[256,1792]{1,0:T(8,128)(2,1)S(1)} %all_gather.25), channel_id=1, source_target_pairs={{0,24},{8,16},{16,8},{24,0},{1,25},{9,17},{17,9},{25,1},{2,26},{10... | collective-permute-start | bytes 2752520 | tf_op jit(solution)/shard_map/ppermute | solution.py:37
  45.1 23.6 %copy-start.4 = (bf16[384,1792]{1,0:T(8,128)(2,1)S(1)}, bf16[384,1792]{1,0:T(8,128)(2,1)}, u32[]{:S(2)}) copy-start(bf16[384,1792]{1,0:T(8,128)(2,1)} %param.7) | copy-start | bytes 4128772
  70.0 7.4 %copy-start = (bf16[384,512]{1,0:T(8,128)(2,1)S(1)}, bf16[384,512]{1,0:T(8,128)(2,1)}, u32[]{:S(2)}) copy-start(bf16[384,512]{1,0:T(8,128)(2,1)} %param.6) | copy-start | bytes 1179652
  71.0 15.9 %all-to-all-start.1 = ((bf16[8,96,256]{2,1,0:T(8,128)(2,1)}), bf16[8,96,256]{2,1,0:T(8,128)(2,1)S(1)}, u32[]{:S(2)}, u32[]{:S(2)}) async-start(bf16[8,96,256]{2,1,0:T(8,128)(2,1)} %bitcast.4), calls=%async_computation.1 | async-start | bytes 786432 | tf_op jit(solution)/shard_map/all_to_all | solution.py:21
  75.2 32.6 %collective-permute-start.3 = (bf16[256,1792]{1,0:T(8,128)(2,1)S(1)}, bf16[256,1792]{1,0:T(8,128)(2,1)}, u32[]{:S(2)}, u32[]{:S(2)}) collective-permute-start(bf16[256,1792]{1,0:T(8,128)(2,1)S(1)} %all_gather.25), channel_id=1, source_target_pairs={{0,8},{8,0},{16,24},{24,16},{1,9},{9,1},{17,25},{25,17},{2,10},{10... | collective-permute-start | bytes 2752520 | tf_op jit(solution)/shard_map/ppermute | solution.py:37
  77.4 29.9 %collective-permute-start.2 = (bf16[384,512]{1,0:T(8,128)(2,1)S(1)}, bf16[384,512]{1,0:T(8,128)(2,1)S(1)}, u32[]{:S(2)}, u32[]{:S(2)}) collective-permute-start(bf16[384,512]{1,0:T(8,128)(2,1)S(1)} %copy-done), channel_id=1, source_target_pairs={{0,8},{8,0},{16,24},{24,16},{1,9},{9,1},{17,25},{25,17},{2,10},{10... | collective-permute-start | bytes 1179656 | tf_op jit(solution)/shard_map/ppermute | solution.py:37
  107.8 11.4 %copy-start.2 = (f32[1,8,1024]{2,1,0:T(8,128)S(1)}, f32[1,8,1024]{2,1,0:T(8,128)}, u32[]{:S(2)}) copy-start(f32[1,8,1024]{2,1,0:T(8,128)} %param.10) | copy-start | bytes 98308
  107.8 11.6 %copy-start.3 = (f32[1,8,1024]{2,1,0:T(8,128)S(1)}, f32[1,8,1024]{2,1,0:T(8,128)}, u32[]{:S(2)}) copy-start(f32[1,8,1024]{2,1,0:T(8,128)} %param.11) | copy-start | bytes 98308
  108.8 27.4 %all-to-all-start.2 = ((bf16[16,32,512]{2,1,0:T(8,128)(2,1)}), bf16[16,32,512]{2,1,0:T(8,128)(2,1)S(1)}, u32[]{:S(2)}, u32[]{:S(2)}) async-start(bf16[16,32,512]{2,1,0:T(8,128)(2,1)} %bitcast.6), calls=%async_computation.2 | async-start | bytes 1048576 | tf_op jit(solution)/shard_map/all_to_all | solution.py:21
  136.9 7.7 %all-to-all-start.3 = ((f32[4,8,512]{2,1,0:T(8,128)}), f32[4,8,512]{2,1,0:T(8,128)S(1)}, u32[]{:S(2)}, u32[]{:S(2)}) async-start(f32[4,8,512]{2,1,0:T(8,128)} %bitcast.7), calls=%async_computation.3 | async-start | bytes 131072 | tf_op jit(solution)/shard_map/all_to_all | solution.py:21
  140.5 24.8 %collective-permute-start.4 = (bf16[256,1792]{1,0:T(8,128)(2,1)S(1)}, bf16[256,1792]{1,0:T(8,128)(2,1)}, u32[]{:S(2)}, u32[]{:S(2)}) collective-permute-start(bf16[256,1792]{1,0:T(8,128)(2,1)S(1)} %collective-permute-done.1), channel_id=1, source_target_pairs={{0,8},{8,0},{16,24},{24,16},{1,9},{9,1},{17,25},{25,17},{2,10},{10... | collective-permute-start | bytes 2752520 | tf_op jit(solution)/shard_map/ppermute | solution.py:37
  148.1 14.8 %all-to-all-start.4 = ((bf16[8,8,1024]{2,1,0:T(8,128)(2,1)}), bf16[8,8,1024]{2,1,0:T(8,128)(2,1)S(1)}, u32[]{:S(2)}, u32[]{:S(2)}) async-start(bf16[8,8,1024]{2,1,0:T(8,128)(2,1)} %broadcast_in_dim.4), calls=%async_computation.4 | async-start | bytes 262144 | tf_op jit(solution)/shard_map/all_to_all | solution.py:21
  163.8 1.5 copy-start.1

commit v6 on v5

--- a/solution.py
+++ b/solution.py
@@ -92,7 +92,7 @@
     owned = jnp.concatenate(
         (jnp.where(low_place, near, far), jnp.where(low_place, far, near)), axis=1
     ).astype(jnp.bfloat16)
-    projected = gather(owned, fsdp)
+    projected = gather(after(owned, act_pair), fsdp)
 
     low = contract(activations, projected[:tokens], ((0,), (0,)))
     low += contract(act_pair, projected[tokens:], ((0,), (0,)))

time: 194 us -> 212 us (1.093)
  waiting for transfers between devices: 30.7 us -> 48.3 us
    ppermute x5, waiting for transfers between devices: 3.46 us -> 20.3 us  [shift(): return lax.ppermute(block, 'x', [(i, j) for i, j in enumerate(pairs)])]
where the time goes in v6:
time: 212 us
  blocking collectives  99.9 us (47%)
  waiting for transfers between devices  48.3 us (23%)
  starting transfers between devices  43 us (20%)
  local copies, waits for them, and re-layouts  8.92 us (4%)
  matrix products  8.22 us (4%)
  other arithmetic  2.24 us (1%)
    all_gather x4, blocking collectives, gather(): return lax.all_gather(block, axes, axis=0, tiled=True)  68.1 us
    all_to_all x4, waiting for transfers between devices, exchange(): return lax.all_to_all(block, axes, 0, 0, tiled=True)  27.9 us
    all_to_all x4, starting transfers between devices, exchange(): return lax.all_to_all(block, axes, 0, 0, tiled=True)  26.7 us
    all_to_all x1, blocking collectives, exchange(): return lax.all_to_all(block, axes, 0, 0, tiled=True)  23.5 us
    ppermute x5, waiting for transfers between devices, shift(): return lax.ppermute(block, 'x', [(i, j) for i, j in enumerate(pairs)])  20.3 us
    ppermute x5, starting transfers between devices, shift(): return lax.ppermute(block, 'x', [(i, j) for i, j in enumerate(pairs)])  16.3 us
    all_gather x2, blocking collectives, shards(): lax.all_gather(column[:, part * 4:part * 4 + 4], 'core', axis=1)  8.33 us
    dot_general x10, matrix products, contract(): lax.dot_general(left, right, (dims, ((), ())), preferred_element_type=jnp...  8.22 us
  transfers between devices with their start and end apart: 9, of which 5 were waited for; matrix products, arithmetic and copies ran while one was open for 6% of the time, Pallas kernels for 0%

profile of v6, /device:TPU:1, one launch (start us, length us, event | category | flops | bytes accessed | tf_op | source)
XLA Modules:
  0.0 211.7 jit_solution(15879849596604831381)
XLA Ops:
  0.6 4.0 %collective-permute-start = (bf16[384,1792]{1,0:T(8,128)(2,1)}, bf16[384,1792]{1,0:T(8,128)(2,1)S(1)}, u32[]{:S(2)}, u32[]{:S(2)}) collective-permute-start(bf16[384,1792]{1,0:T(8,128)(2,1)} %param.7), channel_id=1, source_target_pairs={{0,8},{8,0},{16,24},{24,16},{1,9},{9,1},{17,25},{25,17},{2,10},{10... | collective-permute-start | bytes 4128776 | tf_op jit(solution)/shard_map/ppermute | solution.py:37
  4.6 11.3 %all_gather.24 = bf16[32,1792]{1,0:T(8,128)(2,1)S(1)} all-gather(bf16[16,1792]{1,0:T(8,128)(2,1)} %param.8), channel_id=1, replica_groups=mesh['zh'=2,'y'=8,'x'=4,'zl'=4,'core'=2] {'zh'}, dimensions={0}, use_global_device_ids=true | all-gather | bytes 172032 | tf_op jit(solution)/shard_map/all_gather | solution.py:63
  15.9 23.0 %all_gather.25 = bf16[256,1792]{1,0:T(8,128)(2,1)S(1)} all-gather(bf16[32,1792]{1,0:T(8,128)(2,1)S(1)} %all_gather.24), channel_id=1, replica_groups=mesh['zh'=2,'y'=8,'x'=4,'zl'=4,'core'=2] {'y'}, dimensions={0}, use_global_device_ids=true | all-gather | bytes 1032192 | tf_op jit(solution)/shard_map/all_gather | solution.py:63
  38.9 3.7 %collective-permute-start.1 = (bf16[256,1792]{1,0:T(8,128)(2,1)S(1)}, bf16[256,1792]{1,0:T(8,128)(2,1)S(1)}, u32[]{:S(2)}, u32[]{:S(2)}) collective-permute-start(bf16[256,1792]{1,0:T(8,128)(2,1)S(1)} %all_gather.25), channel_id=1, source_target_pairs={{0,24},{8,16},{16,8},{24,0},{1,25},{9,17},{17,9},{25,1},{2,26},{10... | collective-permute-start | bytes 2752520 | tf_op jit(solution)/shard_map/ppermute | solution.py:37
  42.6 1.9 convolution_convert_fusion.3
  44.5 0.6 convolution_convert_fusion.2
  45.1 23.5 %all_to_all.25 = bf16[8,96,256]{2,1,0:T(8,128)(2,1)S(1)} all-to-all(bf16[8,96,256]{2,1,0:T(8,128)(2,1)S(1)} %bitcast.62), channel_id=1, replica_groups=mesh['zh'=2,'y'=8,'x'=4,'zl'=4,'core'=2] {'zl','core'}, dimensions={0} | all-to-all | bytes 786432 | tf_op jit(solution)/shard_map/all_to_all | solution.py:21
  68.7 0.7 fusion.6
  69.3 0.7 fusion.7
  70.1 0.9 copy.24
  71.0 4.2 %all-to-all-start.1 = ((bf16[8,96,256]{2,1,0:T(8,128)(2,1)}), bf16[8,96,256]{2,1,0:T(8,128)(2,1)S(1)}, u32[]{:S(2)}, u32[]{:S(2)}) async-start(bf16[8,96,256]{2,1,0:T(8,128)(2,1)} %bitcast.4), calls=%async_computation.1 | async-start | bytes 786432 | tf_op jit(solution)/shard_map/all_to_all | solution.py:21
  75.2 2.2 %collective-permute-start.3 = (bf16[256,1792]{1,0:T(8,128)(2,1)S(1)}, bf16[256,1792]{1,0:T(8,128)(2,1)}, u32[]{:S(2)}, u32[]{:S(2)}) collective-permute-start(bf16[256,1792]{1,0:T(8,128)(2,1)S(1)} %all_gather.25), channel_id=1, source_target_pairs={{0,8},{8,0},{16,24},{24,16},{1,9},{9,1},{17,25},{25,17},{2,10},{10... | collective-permute-start | bytes 2752520 | tf_op jit(solution)/shard_map/ppermute | solution.py:37
  77.4 3.1 %collective-permute-start.2 = (bf16[384,512]{1,0:T(8,128)(2,1)S(1)}, bf16[384,512]{1,0:T(8,128)(2,1)S(1)}, u32[]{:S(2)}, u32[]{:S(2)}) collective-permute-start(bf16[384,512]{1,0:T(8,128)(2,1)S(1)} %copy-done), channel_id=1, source_target_pairs={{0,8},{8,0},{16,24},{24,16},{1,9},{9,1},{17,25},{25,17},{2,10},{10... | collective-permute-start | bytes 1179656 | tf_op jit(solution)/shard_map/ppermute | solution.py:37
  80.5 6.4 %all-to-all-done.1 = bf16[8,96,256]{2,1,0:T(8,128)(2,1)S(1)} async-done(((bf16[8,96,256]{2,1,0:T(8,128)(2,1)}), bf16[8,96,256]{2,1,0:T(8,128)(2,1)S(1)}, u32[]{:S(2)}, u32[]{:S(2)}) %all-to-all-start.1) | async-done | bytes 393248 | tf_op jit(solution)/shard_map/all_to_all | solution.py:21
  87.0 20.3 %collective-permute-done.2 = bf16[384,512]{1,0:T(8,128)(2,1)S(1)} collective-permute-done((bf16[384,512]{1,0:T(8,128)(2,1)S(1)}, bf16[384,512]{1,0:T(8,128)(2,1)S(1)}, u32[]{:S(2)}, u32[]{:S(2)}) %collective-permute-start.2) | collective-permute-done | bytes 393248 | tf_op jit(solution)/shard_map/ppermute | solution.py:37
  107.3 16.4 %all_gather.26 = bf16[768,512]{1,0:T(8,128)(2,1)S(1)} all-gather(bf16[96,512]{1,0:T(8,128)(2,1)S(1)} %pad_maximum_fusion.4), channel_id=1, replica_groups=mesh['zh'=2,'y'=8,'x'=4,'zl'=4,'core'=2] {'zl','core'}, dimensions={0}, use_global_device_ids=true | all-gather | bytes 884736 | tf_op jit(solution)/shard_map/all_gather | solution.py:63
  123.8 0.5 fusion.9
  124.2 0.5 fusion.5
  124.7 1.0 copy.25
  125.7 10.3 %all-to-all-start.2 = ((bf16[16,32,512]{2,1,0:T(8,128)(2,1)}), bf16[16,32,512]{2,1,0:T(8,128)(2,1)S(1)}, u32[]{:S(2)}, u32[]{:S(2)}) async-start(bf16[16,32,512]{2,1,0:T(8,128)(2,1)} %bitcast.6), calls=%async_computation.2 | async-start | bytes 1048576 | tf_op jit(solution)/shard_map/all_to_all | solution.py:21
  136.1 0.2 reshape_squeeze.6
  136.3 0.2 reshape_squeeze.7
  136.7 17.1 %all-to-all-done.2 = bf16[16,32,512]{2,1,0:T(8,128)(2,1)S(1)} async-done(((bf16[16,32,512]{2,1,0:T(8,128)(2,1)}), bf16[16,32,512]{2,1,0:T(8,128)(2,1)S(1)}, u32[]{:S(2)}, u32[]{:S(2)}) %all-to-all-start.2) | async-done | bytes 524320 | tf_op jit(solution)/shard_map/all_to_all | solution.py:21
  153.7 0.7 convert_reduce_fusion
  154.5 3.3 %all-to-all-start.3 = ((f32[4,8,512]{2,1,0:T(8,128)}), f32[4,8,512]{2,1,0:T(8,128)S(1)}, u32[]{:S(2)}, u32[]{:S(2)}) async-start(f32[4,8,512]{2,1,0:T(8,128)} %bitcast.7), calls=%async_computation.3 | async-start | bytes 131072 | tf_op jit(solution)/shard_map/all_to_all | solution.py:21
  158.0 3.3 %collective-permute-start.4 = (bf16[256,1792]{1,0:T(8,128)(2,1)S(1)}, bf16[256,1792]{1,0:T(8,128)(2,1)}, u32[]{:S(2)}, u32[]{:S(2)}) collective-permute-start(bf16[256,1792]{1,0:T(8,128)(2,1)S(1)} %collective-permute-done.1), channel_id=1, source_target_pairs={{0,8},{8,0},{16,24},{24,16},{1,9},{9,1},{17,25},{25,17},{2,10},{10... | collective-permute-start | bytes 2752520 | tf_op jit(solution)/shard_map/ppermute | solution.py:37
  161.4 0.8 all-to-all-done.3
  162.2 0.2 add.86
  162.5 0.2 add.87
  162.8 0.7 fusion.11
  164.1 0.3 mul.123
  164.6 0.3 mul.130
  165.0 0.7 broadcast_in_dim.4
  165.7 8.9 %all-to-all-start.4 = ((bf16[8,8,1024]{2,1,0:T(8,128)(2,1)}), bf16[8,8,1024]{2,1,0:T(8,128)(2,1)S(1)}, u32[]{:S(2)}, u32[]{:S(2)}) async-start(bf16[8,8,1024]{2,1,0:T(8,128)(2,1)} %broadcast_in_dim.4), calls=%async_computation.4 | async-start | bytes 262144 | tf_op jit(solution)/shard_map/all_to_all | solution.py:21
  174.6 0.2 maximum_bitcast_fusion.1
  174.8 0.9 broadcast_in_dim_reshape.7
  175.6 0.2 maximum_bitcast_fusion
  175.9 0.9 broadcast_in_dim_reshape.6
  176.7 3.6 %all-to-all-done.4 = bf16[8,8,1024]{2,1,0:T(8,128)(2,1)S(1)} async-done(((bf16[8,8,1024]{2,1,0:T(8,128)(2,1)}), bf16[8,8,1024]{2,1,0:T(8,128)(2,1)S(1)}, u32[]{:S(2)}, u32[]{:S(2)}) %all-to-all-start.4) | async-done | bytes 131104 | tf_op jit(solution)/shard_map/all_to_all | solution.py:21
  180.4 0.3 constant_dynamic-slice_fusion
  180.7 0.3 fusion.23
  181.0 0.3 convolution_add_fusion.2
  181.3 1.5 convolution_add_fusion.1
  182.8 1.5 fusion.3
  184.3 17.4 %all-gather = bf16[32,8,1792]{2,1,0:T(8,128)(2,1)S(1)} all-gather(bf16[8,8,1792]{2,1,0:T(8,128)(2,1)S(1)} %fusion.3), channel_id=2, replica_groups=mesh['zh'=2,'y'=8,'x'=4,'zl'=4,'core'=2] {'zl'}, dimensions={0}, use_global_device_ids=true | all-gather | bytes 1146880 | tf_op jit(solution)/shard_map/all_gather | solution.py:63
  201.8 5.9 %all-gather.1 = bf16[4,8,8,1792]{3,2,1,0:T(8,128)(2,1)S(1)} all-gather(bf16[4,4,8,1792]{3,2,1,0:T(8,128)(2,1)S(1)} %get-tuple-element.9), channel_id=3, replica_groups=mesh['zh'=2,'y'=8,'x'=4,'zl'=4,'core'=2] {'core'}, dimensions={1}, use_global_device_ids=true | all-gather | bytes 1376256 | tf_op jit(solution)/shard_map/all_gather | solution.py:127
  207.7 2.5 %all-gather.2 = bf16[4,8,8,1792]{3,2,1,0:T(8,128)(2,1)S(1)} all-gather(bf16[4,4,8,1792]{3,2,1,0:T(8,128)(2,1)S(1)} %get-tuple-element.10), channel_id=4, replica_groups=mesh['zh'=2,'y'=8,'x'=4,'zl'=4,'core'=2] {'core'}, dimensions={1}, use_global_device_ids=true | all-gather | bytes 1376256 | tf_op jit(solution)/shard_map/all_gather | solution.py:127
  210.3 1.4 copy.27
  (36 shorter events, 1.8 us)
Async XLA Ops:
  0.6 43.9 %collective-permute-start = (bf16[384,1792]{1,0:T(8,128)(2,1)}, bf16[384,1792]{1,0:T(8,128)(2,1)S(1)}, u32[]{:S(2)}, u32[]{:S(2)}) collective-permute-start(bf16[384,1792]{1,0:T(8,128)(2,1)} %param.7), channel_id=1, source_target_pairs={{0,8},{8,0},{16,24},{24,16},{1,9},{9,1},{17,25},{25,17},{2,10},{10... | collective-permute-start | bytes 4128776 | tf_op jit(solution)/shard_map/ppermute | solution.py:37
  38.9 29.8 %collective-permute-start.1 = (bf16[256,1792]{1,0:T(8,128)(2,1)S(1)}, bf16[256,1792]{1,0:T(8,128)(2,1)S(1)}, u32[]{:S(2)}, u32[]{:S(2)}) collective-permute-start(bf16[256,1792]{1,0:T(8,128)(2,1)S(1)} %all_gather.25), channel_id=1, source_target_pairs={{0,24},{8,16},{16,8},{24,0},{1,25},{9,17},{17,9},{25,1},{2,26},{10... | collective-permute-start | bytes 2752520 | tf_op jit(solution)/shard_map/ppermute | solution.py:37
  45.1 23.6 %copy-start.4 = (bf16[384,1792]{1,0:T(8,128)(2,1)S(1)}, bf16[384,1792]{1,0:T(8,128)(2,1)}, u32[]{:S(2)}) copy-start(bf16[384,1792]{1,0:T(8,128)(2,1)} %param.7) | copy-start | bytes 4128772
  70.0 7.4 %copy-start = (bf16[384,512]{1,0:T(8,128)(2,1)S(1)}, bf16[384,512]{1,0:T(8,128)(2,1)}, u32[]{:S(2)}) copy-start(bf16[384,512]{1,0:T(8,128)(2,1)} %param.6) | copy-start | bytes 1179652
  71.0 15.9 %all-to-all-start.1 = ((bf16[8,96,256]{2,1,0:T(8,128)(2,1)}), bf16[8,96,256]{2,1,0:T(8,128)(2,1)S(1)}, u32[]{:S(2)}, u32[]{:S(2)}) async-start(bf16[8,96,256]{2,1,0:T(8,128)(2,1)} %bitcast.4), calls=%async_computation.1 | async-start | bytes 786432 | tf_op jit(solution)/shard_map/all_to_all | solution.py:21
  75.2 49.5 %collective-permute-start.3 = (bf16[256,1792]{1,0:T(8,128)(2,1)S(1)}, bf16[256,1792]{1,0:T(8,128)(2,1)}, u32[]{:S(2)}, u32[]{:S(2)}) collective-permute-start(bf16[256,1792]{1,0:T(8,128)(2,1)S(1)} %all_gather.25), channel_id=1, source_target_pairs={{0,8},{8,0},{16,24},{24,16},{1,9},{9,1},{17,25},{25,17},{2,10},{10... | collective-permute-start | bytes 2752520 | tf_op jit(solution)/shard_map/ppermute | solution.py:37
  77.4 29.9 %collective-permute-start.2 = (bf16[384,512]{1,0:T(8,128)(2,1)S(1)}, bf16[384,512]{1,0:T(8,128)(2,1)S(1)}, u32[]{:S(2)}, u32[]{:S(2)}) collective-permute-start(bf16[384,512]{1,0:T(8,128)(2,1)S(1)} %copy-done), channel_id=1, source_target_pairs={{0,8},{8,0},{16,24},{24,16},{1,9},{9,1},{17,25},{25,17},{2,10},{10... | collective-permute-start | bytes 1179656 | tf_op jit(solution)/shard_map/ppermute | solution.py:37
  124.7 11.4 %copy-start.2 = (f32[1,8,1024]{2,1,0:T(8,128)S(1)}, f32[1,8,1024]{2,1,0:T(8,128)}, u32[]{:S(2)}) copy-start(f32[1,8,1024]{2,1,0:T(8,128)} %param.10) | copy-start | bytes 98308
  124.7 11.6 %copy-start.3 = (f32[1,8,1024]{2,1,0:T(8,128)S(1)}, f32[1,8,1024]{2,1,0:T(8,128)}, u32[]{:S(2)}) copy-start(f32[1,8,1024]{2,1,0:T(8,128)} %param.11) | copy-start | bytes 98308
  125.7 28.0 %all-to-all-start.2 = ((bf16[16,32,512]{2,1,0:T(8,128)(2,1)}), bf16[16,32,512]{2,1,0:T(8,128)(2,1)S(1)}, u32[]{:S(2)}, u32[]{:S(2)}) async-start(bf16[16,32,512]{2,1,0:T(8,128)(2,1)} %bitcast.6), calls=%async_computation.2 | async-start | bytes 1048576 | tf_op jit(solution)/shard_map/all_to_all | solution.py:21
  154.5 7.7 %all-to-all-start.3 = ((f32[4,8,512]{2,1,0:T(8,128)}), f32[4,8,512]{2,1,0:T(8,128)S(1)}, u32[]{:S(2)}, u32[]{:S(2)}) async-start(f32[4,8,512]{2,1,0:T(8,128)} %bitcast.7), calls=%async_computation.3 | async-start | bytes 131072 | tf_op jit(solution)/shard_map/all_to_all | solution.py:21
  158.0 24.8 %collective-permute-start.4 = (bf16[256,1792]{1,0:T(8,128)(2,1)S(1)}, bf16[256,1792]{1,0:T(8,128)(2,1)}, u32[]{:S(2)}, u32[]{:S(2)}) collective-permute-start(bf16[256,1792]{1,0:T(8,128)(2,1)S(1)} %collective-permute-done.1), channel_id=1, source_target_pairs={{0,8},{8,0},{16,24},{24,16},{1,9},{9,1},{17,25},{25,17},{2,10},{10... | collective-permute-start | bytes 2752520 | tf_op jit(solution)/shard_map/ppermute | solution.py:37
  165.7 14.7 %all-to-all-start.4 = ((bf16[8,8,1024]{2,1,0:T(8,128)(2,1)}), bf16[8,8,1024]{2,1,0:T(8,128)(2,1)S(1)}, u32[]{:S(2)}, u32[]{:S(2)}) async-start(bf16[8,8,1024]{2,1,0:T(8,128)(2,1)} %broadcast_in_dim.4), calls=%async_computation.4 | async-start | bytes 262144 | tf_op jit(solution)/shard_map/all_to_all | solution.py:21
  181.3 1.5 copy-start.1

commit v7 on v5

--- a/solution.py
+++ b/solution.py
@@ -86,7 +86,7 @@
 
     near = summed(exchange(project(own), fsdp))
     far = summed(exchange(project(after(other, near)), fsdp))
-    pair_own = shift(own, partner)
+    pair_own = shift(after(own, act_pair), partner)
     pair_other = shift(other, partner)
 
     owned = jnp.concatenate(

time: 194 us -> 196 us (1.010)
  waiting for transfers between devices: 30.7 us -> 34.2 us
    ppermute x5, waiting for transfers between devices: 3.46 us -> 13.1 us  [shift(): return lax.ppermute(block, 'x', [(i, j) for i, j in enumerate(pairs)])]
    all_to_all x4, waiting for transfers between devices: 27.3 us -> 21 us  [exchange(): return lax.all_to_all(block, axes, 0, 0, tiled=True)]
where the time goes in v7:
time: 196 us
  blocking collectives  99.2 us (51%)
  starting transfers between devices  41.8 us (21%)
  waiting for transfers between devices  34.2 us (17%)
  local copies, waits for them, and re-layouts  8.92 us (5%)
  matrix products  8.23 us (4%)
  other arithmetic  2.24 us (1%)
    all_gather x4, blocking collectives, gather(): return lax.all_gather(block, axes, axis=0, tiled=True)  68.8 us
    all_to_all x4, starting transfers between devices, exchange(): return lax.all_to_all(block, axes, 0, 0, tiled=True)  26.4 us
    all_to_all x1, blocking collectives, exchange(): return lax.all_to_all(block, axes, 0, 0, tiled=True)  23.5 us
    all_to_all x4, waiting for transfers between devices, exchange(): return lax.all_to_all(block, axes, 0, 0, tiled=True)  21 us
    ppermute x5, starting transfers between devices, shift(): return lax.ppermute(block, 'x', [(i, j) for i, j in enumerate(pairs)])  15.4 us
    ppermute x5, waiting for transfers between devices, shift(): return lax.ppermute(block, 'x', [(i, j) for i, j in enumerate(pairs)])  13.1 us
    dot_general x10, matrix products, contract(): lax.dot_general(left, right, (dims, ((), ())), preferred_element_type=jnp...  8.23 us
    all_gather x2, blocking collectives, shards(): lax.all_gather(column[:, part * 4:part * 4 + 4], 'core', axis=1)  6.93 us
  transfers between devices with their start and end apart: 9, of which 5 were waited for; matrix products, arithmetic and copies ran while one was open for 6% of the time, Pallas kernels for 0%

profile of v7, /device:TPU:1, one launch (start us, length us, event | category | flops | bytes accessed | tf_op | source)
XLA Modules:
  0.0 195.7 jit_solution(7162753880727211764)
XLA Ops:
  0.6 4.0 %collective-permute-start = (bf16[384,1792]{1,0:T(8,128)(2,1)}, bf16[384,1792]{1,0:T(8,128)(2,1)S(1)}, u32[]{:S(2)}, u32[]{:S(2)}) collective-permute-start(bf16[384,1792]{1,0:T(8,128)(2,1)} %param.7), channel_id=1, source_target_pairs={{0,8},{8,0},{16,24},{24,16},{1,9},{9,1},{17,25},{25,17},{2,10},{10... | collective-permute-start | bytes 4128776 | tf_op jit(solution)/shard_map/ppermute | solution.py:37
  4.6 11.3 %all_gather.24 = bf16[32,1792]{1,0:T(8,128)(2,1)S(1)} all-gather(bf16[16,1792]{1,0:T(8,128)(2,1)} %param.8), channel_id=1, replica_groups=mesh['zh'=2,'y'=8,'x'=4,'zl'=4,'core'=2] {'zh'}, dimensions={0}, use_global_device_ids=true | all-gather | bytes 172032 | tf_op jit(solution)/shard_map/all_gather | solution.py:63
  15.9 23.0 %all_gather.25 = bf16[256,1792]{1,0:T(8,128)(2,1)S(1)} all-gather(bf16[32,1792]{1,0:T(8,128)(2,1)S(1)} %all_gather.24), channel_id=1, replica_groups=mesh['zh'=2,'y'=8,'x'=4,'zl'=4,'core'=2] {'y'}, dimensions={0}, use_global_device_ids=true | all-gather | bytes 1032192 | tf_op jit(solution)/shard_map/all_gather | solution.py:63
  38.9 3.7 %collective-permute-start.1 = (bf16[256,1792]{1,0:T(8,128)(2,1)S(1)}, bf16[256,1792]{1,0:T(8,128)(2,1)S(1)}, u32[]{:S(2)}, u32[]{:S(2)}) collective-permute-start(bf16[256,1792]{1,0:T(8,128)(2,1)S(1)} %all_gather.25), channel_id=1, source_target_pairs={{0,24},{8,16},{16,8},{24,0},{1,25},{9,17},{17,9},{25,1},{2,26},{10... | collective-permute-start | bytes 2752520 | tf_op jit(solution)/shard_map/ppermute | solution.py:37
  42.6 1.9 convolution_convert_fusion.3
  44.5 0.6 convolution_convert_fusion.2
  45.1 23.5 %all_to_all.25 = bf16[8,96,256]{2,1,0:T(8,128)(2,1)S(1)} all-to-all(bf16[8,96,256]{2,1,0:T(8,128)(2,1)S(1)} %bitcast.62), channel_id=1, replica_groups=mesh['zh'=2,'y'=8,'x'=4,'zl'=4,'core'=2] {'zl','core'}, dimensions={0} | all-to-all | bytes 786432 | tf_op jit(solution)/shard_map/all_to_all | solution.py:21
  68.7 0.7 fusion.6
  69.3 0.7 fusion.7
  70.1 0.9 copy.24
  71.0 4.2 %all-to-all-start.1 = ((bf16[8,96,256]{2,1,0:T(8,128)(2,1)}), bf16[8,96,256]{2,1,0:T(8,128)(2,1)S(1)}, u32[]{:S(2)}, u32[]{:S(2)}) async-start(bf16[8,96,256]{2,1,0:T(8,128)(2,1)} %bitcast.4), calls=%async_computation.1 | async-start | bytes 786432 | tf_op jit(solution)/shard_map/all_to_all | solution.py:21
  75.2 2.2 %collective-permute-start.2 = (bf16[384,512]{1,0:T(8,128)(2,1)S(1)}, bf16[384,512]{1,0:T(8,128)(2,1)S(1)}, u32[]{:S(2)}, u32[]{:S(2)}) collective-permute-start(bf16[384,512]{1,0:T(8,128)(2,1)S(1)} %copy-done), channel_id=1, source_target_pairs={{0,8},{8,0},{16,24},{24,16},{1,9},{9,1},{17,25},{25,17},{2,10},{10... | collective-permute-start | bytes 1179656 | tf_op jit(solution)/shard_map/ppermute | solution.py:37
  77.4 10.2 %collective-permute-done.2 = bf16[384,512]{1,0:T(8,128)(2,1)S(1)} collective-permute-done((bf16[384,512]{1,0:T(8,128)(2,1)S(1)}, bf16[384,512]{1,0:T(8,128)(2,1)S(1)}, u32[]{:S(2)}, u32[]{:S(2)}) %collective-permute-start.2) | collective-permute-done | bytes 393248 | tf_op jit(solution)/shard_map/ppermute | solution.py:37
  87.7 2.2 %collective-permute-start.3 = (bf16[256,1792]{1,0:T(8,128)(2,1)S(1)}, bf16[256,1792]{1,0:T(8,128)(2,1)}, u32[]{:S(2)}, u32[]{:S(2)}) collective-permute-start(bf16[256,1792]{1,0:T(8,128)(2,1)S(1)} %all_gather.25), channel_id=1, source_target_pairs={{0,8},{8,0},{16,24},{24,16},{1,9},{9,1},{17,25},{25,17},{2,10},{10... | collective-permute-start | bytes 2752520 | tf_op jit(solution)/shard_map/ppermute | solution.py:37
  90.0 16.7 %all_gather.26 = bf16[768,512]{1,0:T(8,128)(2,1)S(1)} all-gather(bf16[96,512]{1,0:T(8,128)(2,1)S(1)} %pad_maximum_fusion.4), channel_id=1, replica_groups=mesh['zh'=2,'y'=8,'x'=4,'zl'=4,'core'=2] {'zl','core'}, dimensions={0}, use_global_device_ids=true | all-gather | bytes 884736 | tf_op jit(solution)/shard_map/all_gather | solution.py:63
  106.7 0.5 fusion.9
  107.2 0.5 fusion.5
  107.7 2.9 %collective-permute-done.3 = bf16[256,1792]{1,0:T(8,128)(2,1)} collective-permute-done((bf16[256,1792]{1,0:T(8,128)(2,1)S(1)}, bf16[256,1792]{1,0:T(8,128)(2,1)}, u32[]{:S(2)}, u32[]{:S(2)}) %collective-permute-start.3) | collective-permute-done | bytes 917536 | tf_op jit(solution)/shard_map/ppermute | solution.py:37
  110.6 1.0 copy.25
  111.6 10.3 %all-to-all-start.2 = ((bf16[16,32,512]{2,1,0:T(8,128)(2,1)}), bf16[16,32,512]{2,1,0:T(8,128)(2,1)S(1)}, u32[]{:S(2)}, u32[]{:S(2)}) async-start(bf16[16,32,512]{2,1,0:T(8,128)(2,1)} %bitcast.6), calls=%async_computation.2 | async-start | bytes 1048576 | tf_op jit(solution)/shard_map/all_to_all | solution.py:21
  121.9 0.2 reshape_squeeze.6
  122.2 0.2 reshape_squeeze.7
  122.5 16.6 %all-to-all-done.2 = bf16[16,32,512]{2,1,0:T(8,128)(2,1)S(1)} async-done(((bf16[16,32,512]{2,1,0:T(8,128)(2,1)}), bf16[16,32,512]{2,1,0:T(8,128)(2,1)S(1)}, u32[]{:S(2)}, u32[]{:S(2)}) %all-to-all-start.2) | async-done | bytes 524320 | tf_op jit(solution)/shard_map/all_to_all | solution.py:21
  139.1 0.7 convert_reduce_fusion
  139.8 3.3 %all-to-all-start.3 = ((f32[4,8,512]{2,1,0:T(8,128)}), f32[4,8,512]{2,1,0:T(8,128)S(1)}, u32[]{:S(2)}, u32[]{:S(2)}) async-start(f32[4,8,512]{2,1,0:T(8,128)} %bitcast.7), calls=%async_computation.3 | async-start | bytes 131072 | tf_op jit(solution)/shard_map/all_to_all | solution.py:21
  143.4 3.3 %collective-permute-start.4 = (bf16[256,1792]{1,0:T(8,128)(2,1)S(1)}, bf16[256,1792]{1,0:T(8,128)(2,1)}, u32[]{:S(2)}, u32[]{:S(2)}) collective-permute-start(bf16[256,1792]{1,0:T(8,128)(2,1)S(1)} %collective-permute-done.1), channel_id=1, source_target_pairs={{0,8},{8,0},{16,24},{24,16},{1,9},{9,1},{17,25},{25,17},{2,10},{10... | collective-permute-start | bytes 2752520 | tf_op jit(solution)/shard_map/ppermute | solution.py:37
  146.7 0.8 all-to-all-done.3
  147.5 0.2 add.86
  147.8 0.2 add.87
  148.1 0.7 fusion.11
  149.4 0.3 mul.123
  150.0 0.3 mul.130
  150.3 0.7 broadcast_in_dim.4
  151.0 8.6 %all-to-all-start.4 = ((bf16[8,8,1024]{2,1,0:T(8,128)(2,1)}), bf16[8,8,1024]{2,1,0:T(8,128)(2,1)S(1)}, u32[]{:S(2)}, u32[]{:S(2)}) async-start(bf16[8,8,1024]{2,1,0:T(8,128)(2,1)} %broadcast_in_dim.4), calls=%async_computation.4 | async-start | bytes 262144 | tf_op jit(solution)/shard_map/all_to_all | solution.py:21
  159.6 0.2 maximum_bitcast_fusion.1
  159.8 0.9 broadcast_in_dim_reshape.7
  160.7 0.2 maximum_bitcast_fusion
  160.9 0.9 broadcast_in_dim_reshape.6
  161.7 3.6 %all-to-all-done.4 = bf16[8,8,1024]{2,1,0:T(8,128)(2,1)S(1)} async-done(((bf16[8,8,1024]{2,1,0:T(8,128)(2,1)}), bf16[8,8,1024]{2,1,0:T(8,128)(2,1)S(1)}, u32[]{:S(2)}, u32[]{:S(2)}) %all-to-all-start.4) | async-done | bytes 131104 | tf_op jit(solution)/shard_map/all_to_all | solution.py:21
  165.5 0.3 constant_dynamic-slice_fusion
  165.8 0.3 fusion.23
  166.0 0.3 convolution_add_fusion.2
  166.3 1.5 convolution_add_fusion.1
  167.9 1.5 fusion.3
  169.3 17.8 %all-gather = bf16[32,8,1792]{2,1,0:T(8,128)(2,1)S(1)} all-gather(bf16[8,8,1792]{2,1,0:T(8,128)(2,1)S(1)} %fusion.3), channel_id=2, replica_groups=mesh['zh'=2,'y'=8,'x'=4,'zl'=4,'core'=2] {'zl'}, dimensions={0}, use_global_device_ids=true | all-gather | bytes 1146880 | tf_op jit(solution)/shard_map/all_gather | solution.py:63
  187.2 4.5 %all-gather.1 = bf16[4,8,8,1792]{3,2,1,0:T(8,128)(2,1)S(1)} all-gather(bf16[4,4,8,1792]{3,2,1,0:T(8,128)(2,1)S(1)} %get-tuple-element.9), channel_id=3, replica_groups=mesh['zh'=2,'y'=8,'x'=4,'zl'=4,'core'=2] {'core'}, dimensions={1}, use_global_device_ids=true | all-gather | bytes 1376256 | tf_op jit(solution)/shard_map/all_gather | solution.py:127
  191.7 2.5 %all-gather.2 = bf16[4,8,8,1792]{3,2,1,0:T(8,128)(2,1)S(1)} all-gather(bf16[4,4,8,1792]{3,2,1,0:T(8,128)(2,1)S(1)} %get-tuple-element.10), channel_id=4, replica_groups=mesh['zh'=2,'y'=8,'x'=4,'zl'=4,'core'=2] {'core'}, dimensions={1}, use_global_device_ids=true | all-gather | bytes 1376256 | tf_op jit(solution)/shard_map/all_gather | solution.py:127
  194.3 1.4 copy.27
  (36 shorter events, 1.8 us)
Async XLA Ops:
  0.6 43.9 %collective-permute-start = (bf16[384,1792]{1,0:T(8,128)(2,1)}, bf16[384,1792]{1,0:T(8,128)(2,1)S(1)}, u32[]{:S(2)}, u32[]{:S(2)}) collective-permute-start(bf16[384,1792]{1,0:T(8,128)(2,1)} %param.7), channel_id=1, source_target_pairs={{0,8},{8,0},{16,24},{24,16},{1,9},{9,1},{17,25},{25,17},{2,10},{10... | collective-permute-start | bytes 4128776 | tf_op jit(solution)/shard_map/ppermute | solution.py:37
  38.9 29.8 %collective-permute-start.1 = (bf16[256,1792]{1,0:T(8,128)(2,1)S(1)}, bf16[256,1792]{1,0:T(8,128)(2,1)S(1)}, u32[]{:S(2)}, u32[]{:S(2)}) collective-permute-start(bf16[256,1792]{1,0:T(8,128)(2,1)S(1)} %all_gather.25), channel_id=1, source_target_pairs={{0,24},{8,16},{16,8},{24,0},{1,25},{9,17},{17,9},{25,1},{2,26},{10... | collective-permute-start | bytes 2752520 | tf_op jit(solution)/shard_map/ppermute | solution.py:37
  45.1 23.6 %copy-start.4 = (bf16[384,1792]{1,0:T(8,128)(2,1)S(1)}, bf16[384,1792]{1,0:T(8,128)(2,1)}, u32[]{:S(2)}) copy-start(bf16[384,1792]{1,0:T(8,128)(2,1)} %param.7) | copy-start | bytes 4128772
  70.0 5.2 %copy-start = (bf16[384,512]{1,0:T(8,128)(2,1)S(1)}, bf16[384,512]{1,0:T(8,128)(2,1)}, u32[]{:S(2)}) copy-start(bf16[384,512]{1,0:T(8,128)(2,1)} %param.6) | copy-start | bytes 1179652
  71.0 18.9 %all-to-all-start.1 = ((bf16[8,96,256]{2,1,0:T(8,128)(2,1)}), bf16[8,96,256]{2,1,0:T(8,128)(2,1)S(1)}, u32[]{:S(2)}, u32[]{:S(2)}) async-start(bf16[8,96,256]{2,1,0:T(8,128)(2,1)} %bitcast.4), calls=%async_computation.1 | async-start | bytes 786432 | tf_op jit(solution)/shard_map/all_to_all | solution.py:21
  75.2 12.5 %collective-permute-start.2 = (bf16[384,512]{1,0:T(8,128)(2,1)S(1)}, bf16[384,512]{1,0:T(8,128)(2,1)S(1)}, u32[]{:S(2)}, u32[]{:S(2)}) collective-permute-start(bf16[384,512]{1,0:T(8,128)(2,1)S(1)} %copy-done), channel_id=1, source_target_pairs={{0,8},{8,0},{16,24},{24,16},{1,9},{9,1},{17,25},{25,17},{2,10},{10... | collective-permute-start | bytes 1179656 | tf_op jit(solution)/shard_map/ppermute | solution.py:37
  87.7 22.9 %collective-permute-start.3 = (bf16[256,1792]{1,0:T(8,128)(2,1)S(1)}, bf16[256,1792]{1,0:T(8,128)(2,1)}, u32[]{:S(2)}, u32[]{:S(2)}) collective-permute-start(bf16[256,1792]{1,0:T(8,128)(2,1)S(1)} %all_gather.25), channel_id=1, source_target_pairs={{0,8},{8,0},{16,24},{24,16},{1,9},{9,1},{17,25},{25,17},{2,10},{10... | collective-permute-start | bytes 2752520 | tf_op jit(solution)/shard_map/ppermute | solution.py:37
  107.7 14.2 %copy-start.2 = (f32[1,8,1024]{2,1,0:T(8,128)S(1)}, f32[1,8,1024]{2,1,0:T(8,128)}, u32[]{:S(2)}) copy-start(f32[1,8,1024]{2,1,0:T(8,128)} %param.10) | copy-start | bytes 98308
  107.7 14.5 %copy-start.3 = (f32[1,8,1024]{2,1,0:T(8,128)S(1)}, f32[1,8,1024]{2,1,0:T(8,128)}, u32[]{:S(2)}) copy-start(f32[1,8,1024]{2,1,0:T(8,128)} %param.11) | copy-start | bytes 98308
  111.6 27.5 %all-to-all-start.2 = ((bf16[16,32,512]{2,1,0:T(8,128)(2,1)}), bf16[16,32,512]{2,1,0:T(8,128)(2,1)S(1)}, u32[]{:S(2)}, u32[]{:S(2)}) async-start(bf16[16,32,512]{2,1,0:T(8,128)(2,1)} %bitcast.6), calls=%async_computation.2 | async-start | bytes 1048576 | tf_op jit(solution)/shard_map/all_to_all | solution.py:21
  139.8 7.7 %all-to-all-start.3 = ((f32[4,8,512]{2,1,0:T(8,128)}), f32[4,8,512]{2,1,0:T(8,128)S(1)}, u32[]{:S(2)}, u32[]{:S(2)}) async-start(f32[4,8,512]{2,1,0:T(8,128)} %bitcast.7), calls=%async_computation.3 | async-start | bytes 131072 | tf_op jit(solution)/shard_map/all_to_all | solution.py:21
  143.4 24.5 %collective-permute-start.4 = (bf16[256,1792]{1,0:T(8,128)(2,1)S(1)}, bf16[256,1792]{1,0:T(8,128)(2,1)}, u32[]{:S(2)}, u32[]{:S(2)}) collective-permute-start(bf16[256,1792]{1,0:T(8,128)(2,1)S(1)} %collective-permute-done.1), channel_id=1, source_target_pairs={{0,8},{8,0},{16,24},{24,16},{1,9},{9,1},{17,25},{25,17},{2,10},{10... | collective-permute-start | bytes 2752520 | tf_op jit(solution)/shard_map/ppermute | solution.py:37
  151.0 14.4 %all-to-all-start.4 = ((bf16[8,8,1024]{2,1,0:T(8,128)(2,1)}), bf16[8,8,1024]{2,1,0:T(8,128)(2,1)S(1)}, u32[]{:S(2)}, u32[]{:S(2)}) async-start(bf16[8,8,1024]{2,1,0:T(8,128)(2,1)} %broadcast_in_dim.4), calls=%async_computation.4 | async-start | bytes 262144 | tf_op jit(solution)/shard_map/all_to_all | solution.py:21
  166.3 1.5 copy-start.1
